TPU v7x, 32 devices: a whole 2x2x4 slice. The times are simulated.
32 devices in a mesh: ctx: 8 (over y, x, core), ch: 4 (over z).
Axes of the slice: x: 2, y: 2, z: 4, core: 2. Of those that a mesh axis runs over, the one named last changes fastest.
Arguments:
- projected: bfloat16 [3, 4096, 8192], P(None, 'ctx', 'ch'), may hold values from -6 to 6
- short_weight: float32 [3, 3, 8192], P(None, None, 'ch'), may hold values from -3 to 3
- rates: float32 [16, 8192], P(None, 'ch'), may hold values from 6.1035156e-05 to 0.05
- residues: float32 [16, 8192], P(None, 'ch'), may hold values from -1.5 to 1.5
- bias: float32 [8192], P('ch'), may hold values from -3 to 3
- out_weight: bfloat16 [8192, 8192], P('ch', 'ctx'), may hold values from -0.0625 to 0.0625
Outputs:
- layer_out: bfloat16 [4096, 8192], P('ctx', 'ch')
All inputs are finite; a program needn't handle non-finite values.
Results may differ from a plain program's by a relative error of at most 0.018.
Values may be sent and summed in bfloat16 or wider, within the bound.
No kernel may reach another device: no remote copies, remote signals or barrier semaphores. Data moves between devices by JAX's collectives and lax.ppermute only.
A program may use at most 192 MiB of HBM per device.

v0:
```python
import jax
import jax.numpy as jnp
from jax import lax
from jax.sharding import PartitionSpec as P


def from_behind(value, axis, by):
    count = lax.axis_size(axis)
    pairs = [(i, i + by) for i in range(count) if 0 <= i + by < count]
    return lax.ppermute(value, axis, pairs)


def carried_in(value, axis, combine, identity):
    count, mine = (lax.axis_size(axis), lax.axis_index(axis))
    everything = jax.tree.map(
        lambda part, kind: lax.all_gather(part.astype(kind), axis),
        value,
        (jnp.bfloat16, jnp.bfloat16),
    )
    start = jax.tree.map(
        lambda part, zero: jnp.broadcast_to(jnp.asarray(zero, part.dtype), part.shape),
        value,
        identity,
    )

    def step(k, before):
        reached = k < mine
        new = combine(
            before, jax.tree.map(lambda part, own: part[k].astype(own.dtype), everything, value)
        )
        return jax.tree.map(lambda a, b: jnp.where(reached, a, b), new, before)

    return lax.fori_loop(0, count, step, start)


def body(projected, short_weight, rates, residues, bias, out_weight):
    rows_dev = projected.shape[1]
    width_dev = projected.shape[2]
    upper_rows = from_behind(projected[:, rows_dev - 2 :, :], "ctx", 1)
    extended = jnp.concatenate([upper_rows, projected], axis=1).astype(jnp.float32)
    short = short_weight[:, 0, None, :] * extended[:, 2 : 2 + rows_dev, :]
    short = short + short_weight[:, 1, None, :] * extended[:, 1 : 1 + rows_dev, :]
    short = short + short_weight[:, 2, None, :] * extended[:, 0:rows_dev, :]
    gated = (short[1] * short[2]).astype(jnp.bfloat16)
    weighted = residues * jnp.sqrt(2.0 * rates)
    empty = jnp.zeros(rates.shape, jnp.float32)
    span_len = min(128, rows_dev)
    span_count = rows_dev // span_len
    offsets = jnp.arange(span_len, dtype=jnp.float32)
    values = gated.astype(jnp.float32)
    growth = jnp.exp(rates[None] * offsets[:, None, None])
    spread = values.reshape(span_count, span_len, width_dev)[:, :, None, :] * growth[None]
    lower = (offsets[:, None] >= offsets[None, :]).astype(jnp.float32)
    running = jnp.einsum("ts,ksmw->ktmw", lower, spread, precision=lax.Precision.HIGHEST)
    span_end = jnp.exp(-rates * (span_len - 1))[None] * running[:, span_len - 1]
    step_decay = jnp.exp(-rates * span_len)

    def advance(state, ending):
        return (state * step_decay + ending, state)

    local_end, ignored = lax.scan(advance, empty, span_end)

    def combine(earlier, later):
        return (earlier[0] * jnp.exp(-rates * later[1]) + later[0], earlier[1] + later[1])

    entry, length_sum = carried_in(
        (local_end, jnp.full((), float(rows_dev), jnp.float32)),
        "ctx",
        combine,
        (empty, jnp.zeros((), jnp.float32)),
    )
    ignored, starts = lax.scan(advance, entry, span_end)
    totals = running + jnp.exp(-rates)[None, None] * starts[:, None]
    shrink = weighted[None] * jnp.exp(-rates[None] * offsets[:, None, None])
    conv = jnp.sum(shrink[None] * totals, axis=2).reshape(rows_dev, width_dev)
    conv = conv + bias[None, :] * values
    mixed = (short[0] * conv).astype(jnp.bfloat16)
    partials = jnp.dot(
        mixed,
        lax.all_gather(out_weight, "ctx", axis=1, tiled=True),
        preferred_element_type=jnp.float32,
    ).astype(jnp.bfloat16)
    return (
        lax.psum_scatter(partials, "ch", scatter_dimension=1, tiled=True)
        .astype(jnp.float32)
        .astype(jnp.bfloat16)
    )


def solution(mesh):
    in_specs = (
        P(None, "ctx", "ch"),
        P(None, None, "ch"),
        P(None, "ch"),
        P(None, "ch"),
        P("ch"),
        P("ch", "ctx"),
    )
    out_specs = P("ctx", "ch")
    return jax.shard_map(body, mesh=mesh, in_specs=in_specs, out_specs=out_specs, check_vma=False)
```

profile of v0, /device:TPU:0, one launch (start us, length us, event | category | flops | bytes accessed | tf_op | source)
XLA Modules:
  0.0 376.3 jit_solution(4934429450319385447)
XLA Ops:
  6.5 0.7 all-gather.3.cloned.1.call-update
  7.3 0.9 slice.34
  8.2 2.4 collective-permute-start
  10.6 1.2 dynamic-slice
  11.9 0.8 dynamic-update-slice
  12.6 1.1 fusion.17
  13.8 1.1 sqrt_multiply_fusion
  14.8 12.3 %multiply_exponential_fusion = f32[128,16,2048]{2,0,1:T(8,128)} fusion(f32[16,2048]{1,0:T(8,128)} %param.14), kind=kLoop, calls=%fused_computation.12 | loop fusion | flops 4194304 | bytes 16908288 | tf_op jit(solution)/shard_map/exp | solution.py:51
  27.1 7.9 %exponential_multiply_fusion = f32[128,16,2048]{2,0,1:T(8,128)} fusion(f32[16,2048]{1,0:T(8,128)S(1)} %get-tuple-element.397, f32[16,2048]{1,0:T(8,128)S(1)} %get-tuple-element.272), kind=kLoop, calls=%fused_computation.13 | loop fusion | flops 8388608 | bytes 17039360 | tf_op jit(solution)/shard_map/mul | solution.py:74
  35.1 14.7 %all-reduce = bf16[8]{0:T(256)(128)(2,1)S(1)} all-reduce(bf16[8]{0:T(256)(128)(2,1)S(1)} %dynamic-update-slice), channel_id=1, replica_groups=mesh['ctx'=8,'ch'=4] {'ctx'}, use_global_device_ids=true, to_apply=%add | all-reduce | flops 8 | bytes 32
  49.8 9.2 %maximum_convert_fusion = f32[3,514,2048]{2,1,0:T(8,128)} fusion(bf16[3,512,2048]{2,1,0:T(8,128)(2,1)} %param.12, bf16[3,2,2048]{2,1,0:T(2,128)(2,1)S(1)} %collective-permute-done), kind=kLoop, calls=%fused_computation.20 | loop fusion | flops 12632064 | bytes 18948096 | tf_op jit(solution)/shard_map/convert_element_type | solution.py:40
  59.1 24.1 %fusion.8 = f32[3,512,2048]{2,1,0:T(8,128)} fusion(f32[3,514,2048]{2,1,0:T(8,128)} %maximum_convert_fusion, f32[3,2048]{1,0:T(4,128)S(1)} %get-tuple-element.280, f32[3,2048]{1,0:T(4,128)S(1)} %get-tuple-element.281, f32[3,2048]{1,0:T(4,128)S(1)} %bitcast.60), kind=kLoop, calls=%fused_computation.15 | loop fusion | flops 15728640 | bytes 50405376 | tf_op jit(solution)/shard_map/add | solution.py:43
  83.2 5.8 %fusion.14 = f32[1,512,2048]{2,1,0:T(8,128)S(1)} fusion(f32[3,512,2048]{2,1,0:T(8,128)} %fusion.8), kind=kLoop, calls=%fused_computation.28 | loop fusion | flops 3145728 | bytes 12582912 | tf_op jit(solution)/shard_map/convert_element_type | solution.py:50
  89.1 42.9 %fusion.5 = f32[4,128,16,2048]{3,1,2,0:T(8,128)} fusion(f32[128,16,2048]{2,0,1:T(8,128)S(1)} %bitcast.57, f32[4,128,2048]{2,1,0:T(8,128)S(1)} %bitcast.58), kind=kOutput, calls=%fused_computation.11 | convolution fusion | flops 25786597376 | bytes 88080384 | tf_op jit(solution)/shard_map/ts,ksmw->ktmw/dot_general | solution.py:54
  131.9 2.7 slice.50
  134.7 0.2 bitcast_multiply_fusion.1
  134.8 0.3 while.40
  134.9 0.1 bitcast_add_fusion.5
  134.9 0.1 bitcast_add_fusion.5
  135.0 0.1 bitcast_add_fusion.5
  135.2 12.9 %all-gather = bf16[128,2048]{1,0:T(8,128)(2,1)S(1)} all-gather(bf16[16,2048]{1,0:T(8,128)(2,1)S(1)} %convert_element_type.67), channel_id=2, replica_groups=mesh['ctx'=8,'ch'=4] {'ctx'}, dimensions={0}, use_global_device_ids=true | all-gather | bytes 589824 | tf_op jit(solution)/shard_map/all_gather | solution.py:16
  148.1 11.7 %while.41 = (s32[]{:T(128)}, f32[16,2048]{1,0:T(8,128)S(1)}, s32[]{:T(128)}, bf16[8]{0:T(256)(128)(2,1)S(1)}, f32[16,2048]{1,0:T(8,128)S(1)}, /*index=5*/bf16[8,16,2048]{2,1,0:T(8,128)(2,1)S(1)}, s32[]{:T(128)}, s32[]{:T(128)}) while((s32[]{:T(128)}, f32[16,2048]{1,0:T(8,128)S(1)}, s32[]{:T(128)}, bf16[8]{0:T(256)(128)(2,1)S(1)}, ...), condition=%wide.region_3.4_spmd.clone, body=%wide.region_2.3_spmd.clone.sunk | while | flops 196613 | bytes 458879 | solution.py:33
  148.1 0.7 dynamic_slice.38
  149.5 0.1 fusion.21
  149.6 0.7 dynamic_slice.38
  150.9 0.1 fusion.21
  151.0 0.7 dynamic_slice.38
  152.4 0.1 fusion.21
  152.5 0.7 dynamic_slice.38
  153.9 0.1 fusion.21
  154.0 0.7 dynamic_slice.38
  155.3 0.1 fusion.21
  155.4 0.7 dynamic_slice.38
  156.8 0.1 fusion.21
  156.9 0.7 dynamic_slice.38
  158.3 0.1 fusion.21
  158.4 0.7 dynamic_slice.38
  159.7 0.1 fusion.21
  159.8 3.0 while.39
  159.8 0.7 bitcast_dynamic-update-slice_fusion.2
  160.6 0.7 bitcast_dynamic-update-slice_fusion.2
  161.3 0.7 bitcast_dynamic-update-slice_fusion.2
  162.1 0.7 bitcast_dynamic-update-slice_fusion.2
  162.8 1.1 broadcast_multiply_fusion
  163.9 27.1 %multiply_reduce_fusion = f32[4,128,2048]{2,1,0:T(8,128)S(1)} fusion(f32[4,128,16,2048]{3,1,2,0:T(8,128)} %fusion.5, f32[4,16,2048]{2,1,0:T(8,128)S(1)} %broadcast_multiply_fusion, f32[128,16,2048]{2,0,1:T(8,128)} %exponential_multiply_fusion), kind=kLoop, calls=%fused_computation.6 | loop fusion | flops 49283072 | bytes 88604672 | tf_op jit(solution)/shard_map/reduce_sum | solution.py:75
  191.1 7.6 %fusion.12 = bf16[512,2048]{1,0:T(8,128)(2,1)} fusion(f32[3,512,2048]{2,1,0:T(8,128)} %fusion.8, f32[4,128,2048]{2,1,0:T(8,128)S(1)} %multiply_reduce_fusion, f32[2048]{0:T(1024)S(1)} %copy-done), kind=kLoop, calls=%fused_computation.25 | loop fusion | flops 7340032 | bytes 18882560 | tf_op jit(solution)/shard_map/convert_element_type | solution.py:77
  198.7 26.0 %convolution_convert_fusion = bf16[512,8192]{1,0:T(8,128)(2,1)} fusion(bf16[512,2048]{1,0:T(8,128)(2,1)} %fusion.12, bf16[2048,8192]{1,0:T(8,128)(2,1)} %all-gather.3.cloned.1.call-done), kind=kOutput, calls=%fused_computation.19 | convolution fusion | flops 17184063488 | bytes 44040192 | tf_op jit(solution)/shard_map/dot_general | solution.py:78
  224.7 144.8 %reduce-scatter.2.cloned.1.call-done = bf16[512,2048]{1,0:T(8,128)(2,1)} async-done(((bf16[512,8192]{1,0:T(8,128)(2,1)}), bf16[512,2048]{1,0:T(8,128)(2,1)}) %reduce-scatter.2.cloned.1.call-update) | async-done | bytes 2097168 | tf_op jit(solution)/shard_map/reduce_scatter | solution.py:84
  (28 shorter events, 0.4 us)
Async XLA Ops:
  6.5 192.1 %all-gather.3.cloned.1.call-start = ((), (), s32[]{:S(2)}) async-start(), calls=%async_computation.1 | async-start | bytes 37748736 | tf_op jit(solution)/shard_map/all_gather | solution.py:80
  7.3 362.2 %reduce-scatter.2.cloned.1.call-start = ((), (), s32[]{:S(2)}) async-start(), calls=%async_computation.2 | async-start | bytes 10485760 | tf_op jit(solution)/shard_map/reduce_scatter | solution.py:84
  8.2 41.6 %collective-permute-start = (bf16[3,2,2048]{2,1,0:T(2,128)(2,1)S(1)}, bf16[3,2,2048]{2,1,0:T(2,128)(2,1)S(1)}, u32[]{:S(2)}, u32[]{:S(2)}) collective-permute-start(bf16[3,2,2048]{2,1,0:T(2,128)(2,1)S(1)} %slice.34), channel_id=1, source_target_pairs={{0,4},{4,8},{8,12},{12,16},{16,20},{20,24},{24,28},{1,5},{5,9},{9,... | collective-permute-start | bytes 73736 | tf_op jit(solution)/shard_map/ppermute | solution.py:10
  59.0 30.0 %slice-start = ((s8[16777216]{0:T(1024)(128)(4,1)}), s8[4194304]{0:T(1024)(128)(4,1)S(1)}, s32[]{:S(2)}) async-start(s8[16777216]{0:T(1024)(128)(4,1)} %bitcast.56), calls=%async_computation.3 | async-start | bytes 8388608
  59.0 30.0 %slice-start.1 = ((s8[16777216]{0:T(1024)(128)(4,1)}), s8[4194304]{0:T(1024)(128)(4,1)S(1)}, s32[]{:S(2)}) async-start(s8[16777216]{0:T(1024)(128)(4,1)} %bitcast.56), calls=%async_computation.4 | async-start | bytes 8388608
  59.0 30.0 %slice-start.2 = ((s8[16777216]{0:T(1024)(128)(4,1)}), s8[4194304]{0:T(1024)(128)(4,1)S(1)}, s32[]{:S(2)}) async-start(s8[16777216]{0:T(1024)(128)(4,1)} %bitcast.56), calls=%async_computation.5 | async-start | bytes 8388608
  59.0 30.0 %slice-start.3 = ((s8[16777216]{0:T(1024)(128)(4,1)}), s8[4194304]{0:T(1024)(128)(4,1)S(1)}, s32[]{:S(2)}) async-start(s8[16777216]{0:T(1024)(128)(4,1)} %bitcast.56), calls=%async_computation.6 | async-start | bytes 8388608
  163.9 27.2 %copy-start = (f32[2048]{0:T(1024)S(1)}, f32[2048]{0:T(1024)}, u32[]{:S(2)}) copy-start(f32[2048]{0:T(1024)} %param.16) | copy-start | bytes 24580
Sparse Core Ops, SparseCore 0:
  9.3 165.7 all-gather.2
  224.8 144.6 reduce-scatter.1
where the time goes:
time: 377 us; the launch traced here: 376 us
  waiting for transfers between devices  146 us (39%)
  other arithmetic  97.6 us (26%)
  matrix products  68.9 us (18%)
  blocking collectives  27.6 us (7%)
  local copies, waits for them, and re-layouts  14.9 us (4%)
  between operations  13.6 us (4%)
  loops' own time  5.88 us (2%)
    reduce_scatter x1, waiting for transfers between devices, body(): lax.psum_scatter(partials, 'ch', scatter_dimension=1, tiled=True)  145 us
    dot_general x1, matrix products, body(): jnp.einsum('ts,ksmw->ktmw', lower, spread, precision=lax.Precision.HIGHEST)  42.9 us
    reduce_sum x1, other arithmetic, body(): conv = jnp.sum(shrink[None] * totals, axis=2).reshape(rows_dev, width_dev)  27.1 us
    dot_general x1, matrix products, body(): jnp.dot(mixed, lax.all_gather(out_weight, 'ctx', axis=1, tiled=True), pre...  26 us
    add x1, other arithmetic, body(): short = short + short_weight[:, 2, None, :] * extended[:, 0:rows_dev, :]  24.1 us
    unnamed x1, blocking collectives  14.7 us
    all_gather x1, blocking collectives, carried_in(): lax.all_gather(part.astype(kind), axis)  12.9 us
    exp x1, other arithmetic, body(): growth = jnp.exp(rates[None] * offsets[:, None, None])  12.3 us
  transfers between devices with their start and end apart: 3, of which 1 were waited for; matrix products, arithmetic and copies ran while one was open for 41% of the time, Pallas kernels for 0%

commit v1 on v0

v1 whole, which is shorter than its diff:
```python
import functools

import jax
import jax.numpy as jnp
from jax import lax
from jax.experimental import pallas as pl
from jax.experimental.pallas import tpu as pltpu
from jax.sharding import PartitionSpec as P

F32 = jnp.float32
BF16 = jnp.bfloat16
TILES = 4
SUB = 8
LANES = 128
CUTS = 4
VMEM = 63 * 1024 * 1024
SMEM_SPEC = pl.BlockSpec(memory_space=pltpu.SMEM)
ANY_SPEC = pl.BlockSpec(memory_space=pl.ANY)


def swap(value, axis, mask):
    count = lax.axis_size(axis)
    return lax.ppermute(value, axis, [(i, i ^ mask) for i in range(count)])


def from_behind(value, axis):
    count = lax.axis_size(axis)
    return lax.ppermute(value, axis, [(i, i + 1) for i in range(count - 1)])


def spread(row):
    return jnp.broadcast_to(row, (SUB, LANES))


def total(parts):
    parts = list(parts)
    while len(parts) > 1:
        parts = [
            parts[i] + parts[i + 1] if i + 1 < len(parts) else parts[i]
            for i in range(0, len(parts), 2)
        ]
    return parts[0]


def rounded(value):
    return value.astype(BF16).astype(F32)


def cost(micros, moved):
    return pl.CostEstimate(flops=int(micros * 1.0e9), bytes_accessed=int(moved), transcendentals=0)


def params():
    return pltpu.CompilerParams(vmem_limit_bytes=VMEM)


def local_kernel(
    k_ref, v_ref, halo_ref, taps_ref, rates_ref, coef_ref, bias_ref, after_ref,
    y_ref, entry_ref, end_ref, k_rows, v_rows, ends,
):
    rows, width = k_ref.shape[1], k_ref.shape[2]
    order = rates_ref.shape[0]
    length = rows // SUB
    unroll = min(8, length)
    sub = lax.broadcasted_iota(jnp.int32, (SUB, LANES), 0)

    def group(index, _):
        lanes = pl.ds(pl.multiple_of(index * LANES, LANES), LANES)
        k_rows[pl.ds(SUB - 2, 2), :] = halo_ref[1, :, lanes].astype(F32)
        v_rows[pl.ds(SUB - 2, 2), :] = halo_ref[2, :, lanes].astype(F32)
        k_rows[pl.ds(SUB, rows), :] = k_ref[0, :, lanes].astype(F32)
        v_rows[pl.ds(SUB, rows), :] = v_ref[0, :, lanes].astype(F32)
        decay = [spread(jnp.exp(-rates_ref[m : m + 1, lanes])) for m in range(order)]
        coef = [spread(coef_ref[m : m + 1, lanes]) for m in range(order)]
        bias = spread(bias_ref[0:1, lanes])
        kt = [spread(taps_ref[1, j : j + 1, lanes]) for j in range(3)]
        vt = [spread(taps_ref[2, j : j + 1, lanes]) for j in range(3)]

        def pick(ref, b):
            return ref[pl.ds(SUB + b, SUB, stride=length), :]

        def steps(outer, carry):
            k1, k2, v1, v2, state = carry
            for u in range(unroll):
                b = outer * unroll + u
                k0, v0 = pick(k_rows, b), pick(v_rows, b)
                short_k = kt[0] * k0 + kt[1] * k1 + kt[2] * k2
                short_v = vt[0] * v0 + vt[1] * v1 + vt[2] * v2
                gated = rounded(short_k * short_v)
                state = [decay[m] * state[m] + coef[m] * gated for m in range(order)]
                y_ref[b, :, lanes] = total(state + [bias * gated])
                k1, k2, v1, v2 = k0, k1, v0, v1
            return k1, k2, v1, v2, state

        zero = jnp.zeros((SUB, LANES), F32)
        start = (pick(k_rows, -1), pick(k_rows, -2), pick(v_rows, -1), pick(v_rows, -2), [zero] * order)
        state = lax.fori_loop(0, length // unroll, steps, start)[4]
        for m in range(order):
            rate = spread(rates_ref[m : m + 1, lanes])
            scan = state[m]
            reach = 1
            while reach < SUB:
                earlier = pltpu.roll(scan, reach, 0) * jnp.exp(-rate * float(length * reach))
                scan = scan + jnp.where(sub >= reach, earlier, 0.0)
                reach *= 2
            entry_ref[m, :, lanes] = jnp.where(sub >= 1, pltpu.roll(scan, 1, 0), 0.0)
            ends[m : m + 1, :] = scan[SUB - 1 :, :]
        end_ref[:, lanes] = ends[...].astype(end_ref.dtype)
        return 0

    lax.fori_loop(0, width // LANES, group, 0)


def local_part(projected, halo, taps, rates, coef, bias, after):
    rows, width = projected.shape[1:]
    order = rates.shape[0]
    tile = width // TILES
    length = rows // SUB
    return pl.pallas_call(
        local_kernel,
        grid=(width // tile,),
        in_specs=[
            pl.BlockSpec((1, rows, tile), lambda c: (1, 0, c)),
            pl.BlockSpec((1, rows, tile), lambda c: (2, 0, c)),
            pl.BlockSpec((3, 2, tile), lambda c: (0, 0, c)),
            pl.BlockSpec((3, 3, tile), lambda c: (0, 0, c)),
            pl.BlockSpec((order, tile), lambda c: (0, c)),
            pl.BlockSpec((order, tile), lambda c: (0, c)),
            pl.BlockSpec((1, tile), lambda c: (0, c)),
            ANY_SPEC,
        ],
        out_specs=[
            pl.BlockSpec((length, SUB, tile), lambda c: (0, 0, c)),
            pl.BlockSpec((order, SUB, tile), lambda c: (0, 0, c)),
            pl.BlockSpec((order, tile), lambda c: (0, c)),
        ],
        out_shape=[
            jax.ShapeDtypeStruct((length, SUB, width), F32),
            jax.ShapeDtypeStruct((order, SUB, width), F32),
            jax.ShapeDtypeStruct((order, width), BF16),
        ],
        scratch_shapes=[
            pltpu.VMEM((rows + SUB, LANES), F32),
            pltpu.VMEM((rows + SUB, LANES), F32),
            pltpu.VMEM((order, LANES), F32),
        ],
        compiler_params=params(),
        cost_estimate=cost(20, 12 * rows * width),
        name="local_conv",
    )(projected, projected, halo, taps, rates, coef, bias, after)


def mix_kernel(
    count, mine_ref, q_ref, halo_ref, taps_ref, rates_ref, y_ref, entry_ref, ends_ref, *refs
):
    outs, (q_rows, mixed_rows) = refs[-2 - count : -2], refs[-2:]
    rows, width = q_ref.shape[1], q_ref.shape[2]
    order = rates_ref.shape[0]
    length = rows // SUB
    unroll = min(8, length)
    sub = lax.broadcasted_iota(jnp.int32, (SUB, LANES), 0).astype(F32)

    def group(index, _):
        lanes = pl.ds(pl.multiple_of(index * LANES, LANES), LANES)
        rates = rates_ref[:, lanes]
        across = jnp.exp(-rates * float(rows))
        before = jnp.zeros((order, LANES), F32)
        for device in range(ends_ref.shape[0] - 1):
            later = before * across + ends_ref[device, :, lanes].astype(F32)
            before = jnp.where(device < mine_ref[0], later, before)
        q_rows[pl.ds(SUB - 2, 2), :] = halo_ref[0, :, lanes].astype(F32)
        q_rows[pl.ds(SUB, rows), :] = q_ref[0, :, lanes].astype(F32)
        decay, carried = [], []
        for m in range(order):
            rate = spread(rates[m : m + 1, :])
            decay.append(jnp.exp(-rate))
            at_entry = entry_ref[m, :, lanes] + spread(before[m : m + 1, :]) * jnp.exp(
                -rate * (sub * float(length))
            )
            carried.append(at_entry * decay[m])
        qt = [spread(taps_ref[0, j : j + 1, lanes]) for j in range(3)]

        def pick(b):
            return q_rows[pl.ds(SUB + b, SUB, stride=length), :]

        def steps(outer, carry):
            q1, q2, carried = carry
            for u in range(unroll):
                b = outer * unroll + u
                q0 = pick(b)
                short_q = qt[0] * q0 + qt[1] * q1 + qt[2] * q2
                conv = y_ref[b, :, lanes] + total(carried)
                mixed_rows[pl.ds(b, SUB, stride=length), :] = short_q * conv
                carried = [carried[m] * decay[m] for m in range(order)]
                q1, q2 = q0, q1
            return q1, q2, carried

        lax.fori_loop(0, length // unroll, steps, (pick(-1), pick(-2), carried))
        for step, out in enumerate(outs):

            @pl.when(pl.program_id(0) == step)
            def _():
                out[:, lanes] = mixed_rows[...].astype(out.dtype)

        return 0

    lax.fori_loop(0, width // LANES, group, 0)


def mix_part(mine, projected, halo, taps, rates, y, entry, ends, tiles, after):
    rows, width = projected.shape[1:]
    order = rates.shape[0]
    tile = width // TILES
    length = rows // SUB
    first, count = tiles[0], len(tiles)
    return pl.pallas_call(
        functools.partial(mix_kernel, count),
        grid=(count,),
        in_specs=[
            SMEM_SPEC,
            pl.BlockSpec((1, rows, tile), lambda c: (0, 0, first + c)),
            pl.BlockSpec((3, 2, tile), lambda c: (0, 0, first + c)),
            pl.BlockSpec((3, 3, tile), lambda c: (0, 0, first + c)),
            pl.BlockSpec((order, tile), lambda c: (0, first + c)),
            pl.BlockSpec((length, SUB, tile), lambda c: (0, 0, first + c)),
            pl.BlockSpec((order, SUB, tile), lambda c: (0, 0, first + c)),
            pl.BlockSpec((ends.shape[0], order, tile), lambda c: (0, 0, first + c)),
        ] + [ANY_SPEC] * len(after),
        out_specs=[pl.BlockSpec((rows, tile), lambda c: (0, 0))] * count,
        out_shape=[jax.ShapeDtypeStruct((rows, tile), BF16)] * count,
        scratch_shapes=[
            pltpu.VMEM((rows + SUB, LANES), F32),
            pltpu.VMEM((rows, LANES), F32),
        ],
        compiler_params=params(),
        cost_estimate=cost(20, 8),
        name="mix",
    )(mine, projected, halo, taps, rates, y, entry, ends, *after)


def join_kernel(*refs):
    pass


def join_part(value, after):
    return pl.pallas_call(
        join_kernel,
        in_specs=[ANY_SPEC] * (1 + len(after)),
        out_specs=ANY_SPEC,
        out_shape=jax.ShapeDtypeStruct(value.shape, value.dtype),
        input_output_aliases={0: 0},
        cost_estimate=cost(0.1, 8),
        name="join",
    )(value, *after)


def copy_kernel(places, *refs):
    count = len(places)
    outs, stages, sems = refs[-2 * count - 1 : -count - 1], refs[-count - 1 : -1], refs[-1]
    moves = []
    for i, (rows, cols) in enumerate(places):
        size = rows[1] // CUTS
        for j in range(CUTS):
            here = pl.ds(j * size, size)
            there = refs[i].at[pl.ds(rows[0] + j * size, size), pl.ds(*cols)]
            moves.append((
                pltpu.make_async_copy(there, stages[i].at[here], sems.at[0, i, j]),
                pltpu.make_async_copy(stages[i].at[here], outs[i].at[here], sems.at[1, i, j]),
            ))
    for load, _ in moves:
        load.start()
    for load, store in moves:
        load.wait()
        store.start()
    for _, store in moves:
        store.wait()


def copy_part(sources, after, name):
    arrays = [array for array, _, _ in sources]
    places = [(rows, cols) for _, rows, cols in sources]
    out_shape = [jax.ShapeDtypeStruct((rows[1], cols[1]), a.dtype) for a, rows, cols in sources]
    return pl.pallas_call(
        functools.partial(copy_kernel, places),
        in_specs=[ANY_SPEC] * (len(arrays) + len(after)),
        out_specs=[ANY_SPEC] * len(out_shape),
        out_shape=out_shape,
        scratch_shapes=[pltpu.VMEM((rows[1], cols[1]), a.dtype) for a, rows, cols in sources]
        + [pltpu.SemaphoreType.DMA((2, len(sources), CUTS))],
        compiler_params=params(),
        cost_estimate=cost(0.1, 8),
        name=name,
    )(*arrays, *after)


def project_kernel(parts, slot_ref, *refs):
    sides = [
        jnp.concatenate([ref[...] for ref in refs[side * TILES : (side + 1) * TILES]], axis=1)
        for side in range(2)
    ]
    refs = refs[2 * TILES :]
    weights, (after_ref, out_ref, token_ref) = refs[: sum(parts)], refs[sum(parts) :]
    token_ref[...] = jnp.zeros(token_ref.shape, F32)
    at = 0
    for piece, count in enumerate(parts):
        for side, tokens in enumerate(sides):
            result = None
            low = 0
            for part in weights[at : at + count]:
                depth = part.shape[0]
                term = jnp.dot(tokens[:, low : low + depth], part[...], preferred_element_type=F32)
                result = term if result is None else result + term
                low += depth
            out_ref[piece ^ slot_ref[0], side] = result.astype(BF16)
        at += count


def project_part(slot, own, other, pieces, first, width, weight, after):
    rows, depth = own[0].shape
    parts = [len(piece) for piece in pieces]
    weights = [part for piece in pieces for part in piece]
    steps = 2
    tile = rows // steps
    in_specs = [SMEM_SPEC] + [pl.BlockSpec((tile, depth), lambda i: (i, 0))] * (2 * TILES)
    for i, part in enumerate(weights):
        if i == 0:
            in_specs.append(
                pl.BlockSpec((pl.Element(part.shape[0]), pl.Element(width)), lambda i: (0, first))
            )
        else:
            in_specs.append(pl.BlockSpec(part.shape, lambda i: (0, 0)))
    count = len(pieces)
    return pl.pallas_call(
        functools.partial(project_kernel, parts),
        grid=(steps,),
        in_specs=in_specs + [ANY_SPEC],
        out_specs=[
            pl.BlockSpec((count, 2, tile, width), lambda i: (0, 0, i, 0)),
            pl.BlockSpec((SUB, LANES), lambda i: (0, 0)),
        ],
        out_shape=[
            jax.ShapeDtypeStruct((count, 2, rows, width), BF16),
            jax.ShapeDtypeStruct((SUB, LANES), F32),
        ],
        compiler_params=params(),
        cost_estimate=cost(weight, 8),
        name="project",
    )(slot, *own, *other, *weights, after)


def place_kernel(side_ref, *refs):
    refs[-1][...] = refs[0][...]


def place_both_kernel(side_ref, sums_ref, *refs):
    refs[-2][...] = sums_ref[0]
    refs[-1][...] = sums_ref[1]


def place_part(side, sums, landed, first, out, shape):
    rows, half = shape[0], shape[1] // 2 // LANES
    strip = sums if landed is None else landed
    width = strip.shape[-1]

    def column(i, side_ref):
        which = side_ref[0] if landed is None else 1 - side_ref[0]
        return (0, which * half + first // LANES + i)

    if landed is None:
        in_specs = [pl.BlockSpec((2, rows, LANES), lambda i, side_ref: (0, 0, i))]
    else:
        in_specs = [pl.BlockSpec((rows, LANES), lambda i, side_ref: (0, i))]
    out_specs = [pl.BlockSpec((rows, LANES), column)]
    out_shape = [jax.ShapeDtypeStruct(shape, BF16)]
    if landed is None:
        out_specs.append(pl.BlockSpec((rows, LANES), lambda i, side_ref: (0, i)))
        out_shape.append(jax.ShapeDtypeStruct((rows, width), BF16))
    args, aliases = [strip], {}
    if out is not None:
        aliases = {2: 0}
        in_specs.append(ANY_SPEC)
        args.append(out)
    return pl.pallas_call(
        place_both_kernel if landed is None else place_kernel,
        grid_spec=pltpu.PrefetchScalarGridSpec(
            num_scalar_prefetch=1,
            grid=(width // LANES,),
            in_specs=in_specs,
            out_specs=out_specs,
        ),
        out_shape=out_shape,
        input_output_aliases=aliases,
        compiler_params=params(),
        cost_estimate=cost(0.2, 8),
        name="place",
    )(side, *args)


def body(projected, short_weight, rates, residues, bias, out_weight):
    rows, width = projected.shape[1:]
    depth, columns = out_weight.shape
    count = lax.axis_size("ctx")
    groups = lax.axis_size("ch")
    per = count // groups
    assert per == 2
    mine = lax.axis_index("ctx")
    slot = ((mine // per) ^ lax.axis_index("ch")).astype(jnp.int32)[None]
    coef = residues * jnp.sqrt(2.0 * rates)
    near, far = 2, 4
    more = [1 << b for b in range(3, 16) if 1 << b < count]

    units = columns // LANES
    first = max(units // 4, 1)
    second = (units - first + 1) // 2
    widths = [LANES * part for part in (first, second, units - first - second)]
    starts = [sum(widths[:s]) for s in range(len(widths))]
    stages = len(widths)

    def cut_of(s):
        return (out_weight, (0, depth), (starts[s], widths[s]))

    def first_hops(sent):
        return swap(sent, "ctx", near), swap(sent, "ctx", far)

    def second_hops(s, arrived, after, then=True):
        half, cols = depth // 2, (0, widths[s])
        sources = [(arrived[0], (0, half), cols), (arrived[1], (half, half), cols)]
        if then and s + 1 < stages:
            sources.append(cut_of(s + 1))
        low, high, *sent = copy_part(sources, after, "pass_weights")
        diagonal = [swap(low, "ctx", far), swap(high, "ctx", near)]
        return low, diagonal, first_hops(sent[0]) if sent else None

    def pieces_of(s, arrived, diagonal):
        pieces = {
            0: [out_weight],
            near: [arrived[0]],
            far: [arrived[1]],
            near | far: list(diagonal),
        }
        for mask in more:
            for r, parts in list(pieces.items()):
                if r == 0:
                    parts = [out_weight[:, starts[s] : starts[s] + widths[s]]]
                pieces[r ^ mask] = [swap(part, "ctx", mask) for part in parts]
        return [pieces[r] for r in sorted(pieces)]

    halo = from_behind(projected[:, rows - 2 :, :], "ctx")
    (sent,) = copy_part([cut_of(0)], [halo], "cut")
    arrived = first_hops(sent)
    y, entry, end = local_part(projected, halo, short_weight, rates, coef, bias[None], sent)
    ends = lax.all_gather(join_part(end, arrived), "ctx")
    token, diagonal, _ = second_hops(0, arrived, [ends], then=False)
    mixed, other = [], []
    for tiles in (range(TILES // 2), range(TILES // 2, TILES)):
        made = mix_part(
            mine.astype(jnp.int32)[None], projected, halo, short_weight, rates, y, entry, ends, tiles,
            [token, *(diagonal if mixed else ())],
        )
        if not mixed:
            (token,) = copy_part([cut_of(1)], [made[0]], "cut")
            upcoming = first_hops(token)
        mixed += made
        other += [swap(part, "ctx", 1) for part in made]
    token = mixed[-1]
    slot = (mine // per).astype(jnp.int32)[None]
    side = (mine % per).astype(jnp.int32)[None]
    shape = (rows, per * columns)
    sums = []

    def place_stage(s, out):
        out, given = place_part(side, sums[s], None, starts[s], out, shape)
        return place_part(side, None, swap(given, "ctx", 1), starts[s], out, shape)[0]

    for s in range(stages):
        if s > 0:
            arrived = upcoming
            token, diagonal, upcoming = second_hops(s, arrived, [token, *sums[: s - 1]])
        pieces = pieces_of(s, arrived, diagonal)
        partial, token = project_part(
            slot, mixed, other, pieces, starts[s], widths[s], (0.1, 35, 50)[s], token
        )
        if s == stages - 1:
            out = place_stage(0, None)
            partial = join_part(partial, [sums[-1], out])
        elif s > 0:
            partial = join_part(partial, sums[-1:])
        sums.append(lax.psum_scatter(partial, "ch", scatter_dimension=0))
    for s in range(1, stages):
        out = place_stage(s, out)
    return out


def solution(mesh):
    in_specs = (
        P(None, "ctx", "ch"),
        P(None, None, "ch"),
        P(None, "ch"),
        P(None, "ch"),
        P("ch"),
        P("ch", "ctx"),
    )
    out_specs = P("ctx", "ch")
    return jax.shard_map(body, mesh=mesh, in_specs=in_specs, out_specs=out_specs, check_vma=False)
```

time: 377 us -> 284 us (0.75)
  Pallas kernels: 0 us -> 97.2 us
  other arithmetic: 97.6 us -> 1.66 us
  matrix products: 68.9 us -> 0 us
  starting transfers between devices: 2.4 us -> 19.2 us
  blocking collectives: 27.6 us -> 10.9 us
  local copies, waits for them, and re-layouts: 14.9 us -> 3.78 us
  waiting for transfers between devices: 146 us -> 137 us
  loops' own time: 5.88 us -> 0 us
    pallas_call x0 -> x20, Pallas kernels: none -> 97.2 us  [the longest x3 36.8 us: project_part(): pl.pallas_call(functools.partial(project_kernel, parts), grid=(steps,), i...]
    reduce_scatter x1 -> x3, waiting for transfers between devices: 145 us -> 62.6 us  [body(): sums.append(lax.psum_scatter(partial, 'ch', scatter_dimension=0))]
    ppermute x1 -> x20, waiting for transfers between devices: 0.01 us -> 74.2 us  [the longest x19 74.2 us: swap(): return lax.ppermute(value, axis, [(i, i ^ mask) for i in range(count)])]
    dot_general x2 -> x0, matrix products: 68.9 us -> none  [the longest x1 42.9 us: body(): jnp.einsum('ts,ksmw->ktmw', lower, spread, precision=lax.Precision.HIGHEST)]
    reduce_sum x1 -> x0, other arithmetic: 27.1 us -> none  [body(): conv = jnp.sum(shrink[None] * totals, axis=2).reshape(rows_dev, width_dev)]
    add x9 -> x0, other arithmetic: 24.6 us -> none  [the longest x1 24.1 us: body(): short = short + short_weight[:, 2, None, :] * extended[:, 0:rows_dev, :]]
    convert_element_type x4 -> x0, other arithmetic: 22.7 us -> none  [the longest x1 9.25 us: body(): jnp.concatenate([upper_rows, projected], axis=1).astype(jnp.float32)]
    ppermute x1 -> x20, starting transfers between devices: 2.36 us -> 18.9 us  [the longest x19 16.5 us: swap(): return lax.ppermute(value, axis, [(i, i ^ mask) for i in range(count)])]
  transfers between devices with their start and end apart: 3 -> 23, of which waited for: 1 -> 18; matrix products, arithmetic and copies ran while one was open for 41% -> 1% of each run, Pallas kernels for 0% -> 31%
where the time goes in v1:
time: 284 us; the launch traced here: 283 us
  waiting for transfers between devices  137 us (48%)
  Pallas kernels  97.2 us (34%)
  starting transfers between devices  19.2 us (7%)
  between operations  13.2 us (5%)
  blocking collectives  10.9 us (4%)
  local copies, waits for them, and re-layouts  3.78 us (1%)
    ppermute x19, waiting for transfers between devices, swap(): return lax.ppermute(value, axis, [(i, i ^ mask) for i in range(count)])  74.2 us
    reduce_scatter x3, waiting for transfers between devices, body(): sums.append(lax.psum_scatter(partial, 'ch', scatter_dimension=0))  62.6 us
    pallas_call x3, Pallas kernels, project_part(): pl.pallas_call(functools.partial(project_kernel, parts), grid=(steps,), i...  36.8 us
    pallas_call x1, Pallas kernels, local_part(): pl.pallas_call(local_kernel, grid=(width // tile,), in_specs=[pl.BlockSpe...  20.1 us
    ppermute x19, starting transfers between devices, swap(): return lax.ppermute(value, axis, [(i, i ^ mask) for i in range(count)])  16.5 us
    pallas_call x6, Pallas kernels, place_part(): pl.pallas_call(place_both_kernel if landed is None else place_kernel, gri...  14.4 us
    pallas_call x2, Pallas kernels, mix_part(): pl.pallas_call(functools.partial(mix_kernel, count), grid=(count,), in_sp...  13.9 us
    pallas_call x5, Pallas kernels, copy_part(): pl.pallas_call(functools.partial(copy_kernel, places), in_specs=[ANY_SPEC...  12.1 us
  transfers between devices with their start and end apart: 23, of which 18 were waited for; matrix products, arithmetic and copies ran while one was open for 1% of the time, Pallas kernels for 31%

profile of v1, /device:TPU:0, one launch (start us, length us, event | category | flops | bytes accessed | tf_op | source)
XLA Modules:
  0.0 282.9 jit_solution(8177212641766192145)
XLA Ops:
  6.5 0.9 slice.3
  7.5 2.4 collective-permute-start
  9.8 1.7 sqrt_multiply_fusion.coef_ref
  11.5 0.6 copy-done.4
  12.1 2.0 cut.2.after_ref
  14.1 4.1 %collective-permute-start.1 = (bf16[2048,256]{1,0:T(8,128)(2,1)}, bf16[2048,256]{1,0:T(8,128)(2,1)}, u32[]{:S(2)}, u32[]{:S(2)}) collective-permute-start(bf16[2048,256]{1,0:T(8,128)(2,1)} %cut.2.after_ref), channel_id=1, source_target_pairs={{0,8},{4,12},{8,0},{12,4},{16,24},{20,28},{24,16},{28,20},{1,9},{5... | collective-permute-start | bytes 3145736 | tf_op jit(solution)/shard_map/ppermute | solution.py:23
  18.2 1.5 collective-permute-start.2
  19.7 20.1 %local_conv.1 = (f32[64,8,2048]{2,1,0:T(8,128)}, f32[16,8,2048]{2,1,0:T(8,128)}, bf16[16,2048]{1,0:T(8,128)(2,1)}) custom-call(bf16[3,512,2048]{2,1,0:T(8,128)(2,1)} %q_ref.3, bf16[3,512,2048]{2,1,0:T(8,128)(2,1)} %q_ref.3, bf16[3,2,2048]{2,1,0:T(2,128)(2,1)} %copy-done.4, f32[3,3,2048]{2,1,0:T(4,128)} %taps_ref.5, f32[16,2048]{1,0:T(8,128)} %rates_ref.5, ...), custom_call_target="tpu_custom_call" | custom-call | flops 20000000000 | bytes 12582912 | tf_op jit(solution)/shard_map/local_conv/pallas_call | solution.py:119
  39.8 2.3 collective-permute-done.1.refs_1_.refs_0_.refs_9_
  42.1 1.2 collective-permute-done.2.refs_2_.refs_1_.refs_10_
  43.3 10.9 %all-gather = bf16[128,2048]{1,0:T(8,128)(2,1)} all-gather(bf16[16,2048]{1,0:T(8,128)(2,1)} %join.3), channel_id=2, replica_groups=mesh['ctx'=8,'ch'=4] {'ctx'}, dimensions={0}, use_global_device_ids=true | all-gather | bytes 589824 | tf_op jit(solution)/shard_map/all_gather | solution.py:452
  54.3 2.1 pass_weights.3
  56.9 1.6 collective-permute-start.4
  58.5 7.0 %mix.2 = (bf16[512,512]{1,0:T(8,128)(2,1)}, bf16[512,512]{1,0:T(8,128)(2,1)}) custom-call(s32[1]{0:T(128)} %bitcast.2.mine_ref, bf16[3,512,2048]{2,1,0:T(8,128)(2,1)} %q_ref.3, bf16[3,2,2048]{2,1,0:T(2,128)(2,1)} %copy-done.4, f32[3,3,2048]{2,1,0:T(4,128)} %taps_ref.5, f32[16,2048]{1,0:T(8,128)} %rates_ref.5, f32[64,8,2048]{2,1,0:T(8,128)} %get-tuple-element.30.y_ref, ...), custom_call_target="tpu_custom_call" | custom-call | flops 20000000000 | bytes 8 | tf_op jit(solution)/shard_map/mix/pallas_call | solution.py:216
  65.4 2.3 cut.3.refs_0_
  68.2 1.6 collective-permute-start.9
  69.8 1.1 collective-permute-done.3.refs_1_.refs_11_
  71.1 6.9 %mix.3 = (bf16[512,512]{1,0:T(8,128)(2,1)}, bf16[512,512]{1,0:T(8,128)(2,1)}) custom-call(s32[1]{0:T(128)} %bitcast.2.mine_ref, bf16[3,512,2048]{2,1,0:T(8,128)(2,1)} %q_ref.3, bf16[3,2,2048]{2,1,0:T(2,128)(2,1)} %copy-done.4, f32[3,3,2048]{2,1,0:T(4,128)} %taps_ref.5, f32[16,2048]{1,0:T(8,128)} %rates_ref.5, f32[64,8,2048]{2,1,0:T(8,128)} %get-tuple-element.30.y_ref, ...), custom_call_target="tpu_custom_call" | custom-call | flops 20000000000 | bytes 8 | tf_op jit(solution)/shard_map/mix/pallas_call | solution.py:216
  78.5 1.7 collective-permute-done.7.refs_6_
  80.3 0.7 collective-permute-done.8.refs_7_
  81.0 8.7 %project.3 = (bf16[4,2,512,256]{3,2,1,0:T(8,128)(2,1)}, f32[8,128]{1,0:T(8,128)}) custom-call(s32[1]{0:T(128)} %bitcast.1.slot_ref, bf16[512,512]{1,0:T(8,128)(2,1)} %get-tuple-element.34.refs_1_.refs_0_, bf16[512,512]{1,0:T(8,128)(2,1)} %get-tuple-element.35.refs_1_, bf16[512,512]{1,0:T(8,128)(2,1)} %get-tuple-element.37.refs_2_, ...), custom_call_target="tpu_custom_call" | custom-call | flops 100000000 | bytes 8 | tf_op jit(solution)/shard_map/project/pallas_call | solution.py:333
  89.9 15.0 %collective-permute-done.10.refs_1_.refs_10_ = bf16[2048,384]{1,0:T(8,128)(2,1)} collective-permute-done((bf16[2048,384]{1,0:T(8,128)(2,1)}, bf16[2048,384]{1,0:T(8,128)(2,1)}, u32[]{:S(2)}, u32[]{:S(2)}) %collective-permute-start.10) | collective-permute-done | bytes 1572896 | tf_op jit(solution)/shard_map/ppermute | solution.py:23
  105.0 3.4 %pass_weights.4 = (bf16[1024,384]{1,0:T(8,128)(2,1)}, bf16[1024,384]{1,0:T(8,128)(2,1)}, bf16[2048,384]{1,0:T(8,128)(2,1)}) custom-call(bf16[2048,384]{1,0:T(8,128)(2,1)} %collective-permute-done.9.refs_0_.refs_9_, bf16[2048,384]{1,0:T(8,128)(2,1)} %collective-permute-done.10.refs_1_.refs_10_, bf16[2048,1024]{1,0:T(8,128)(2,1)} %refs_8_.5, ...), custom_call_target="tpu_custom_call" | custom-call | flops 100000000 | bytes 8 | tf_op jit(solution)/shard_map/pass_weights/pallas_call | solution.py:283
  108.4 1.6 collective-permute-start.13
  110.3 1.7 collective-permute-start.11
  112.5 16.6 %collective-permute-done.13.refs_11_ = bf16[1024,384]{1,0:T(8,128)(2,1)S(1)} collective-permute-done((bf16[1024,384]{1,0:T(8,128)(2,1)}, bf16[1024,384]{1,0:T(8,128)(2,1)S(1)}, u32[]{:S(2)}, u32[]{:S(2)}) %collective-permute-start.13) | collective-permute-done | bytes 786464 | tf_op jit(solution)/shard_map/ppermute | solution.py:23
  129.1 1.7 collective-permute-done.14.refs_12_
  130.8 14.0 %project.4 = (bf16[4,2,512,384]{3,2,1,0:T(8,128)(2,1)}, f32[8,128]{1,0:T(8,128)}) custom-call(s32[1]{0:T(128)} %bitcast.1.slot_ref, bf16[512,512]{1,0:T(8,128)(2,1)} %get-tuple-element.34.refs_1_.refs_0_, bf16[512,512]{1,0:T(8,128)(2,1)} %get-tuple-element.35.refs_1_, bf16[512,512]{1,0:T(8,128)(2,1)} %get-tuple-element.37.refs_2_, ...), custom_call_target="tpu_custom_call" | custom-call | flops 35000000512 | bytes 8 | tf_op jit(solution)/shard_map/project/pallas_call | solution.py:333
  145.1 17.4 %collective-permute-done.11.refs_0_.refs_9_ = bf16[2048,384]{1,0:T(8,128)(2,1)} collective-permute-done((bf16[2048,384]{1,0:T(8,128)(2,1)}, bf16[2048,384]{1,0:T(8,128)(2,1)}, u32[]{:S(2)}, u32[]{:S(2)}) %collective-permute-start.11) | collective-permute-done | bytes 1572896 | tf_op jit(solution)/shard_map/ppermute | solution.py:23
  162.6 2.4 pass_weights.5
  164.9 0.6 collective-permute-start.15
  165.6 1.4 collective-permute-start.16
  167.0 1.8 place.6
  168.8 1.7 collective-permute-done.17.refs_0_
  170.5 0.7 copy-done.3
  171.3 1.6 place.7.refs_2_.refs_0_
  172.9 10.0 %collective-permute-done.15.refs_11_ = bf16[1024,384]{1,0:T(8,128)(2,1)} collective-permute-done((bf16[1024,384]{1,0:T(8,128)(2,1)}, bf16[1024,384]{1,0:T(8,128)(2,1)}, u32[]{:S(2)}, u32[]{:S(2)}) %collective-permute-start.15) | collective-permute-done | bytes 786464 | tf_op jit(solution)/shard_map/ppermute | solution.py:23
  183.4 14.0 %project.5 = (bf16[4,2,512,384]{3,2,1,0:T(8,128)(2,1)}, f32[8,128]{1,0:T(8,128)}) custom-call(s32[1]{0:T(128)} %bitcast.1.slot_ref, bf16[512,512]{1,0:T(8,128)(2,1)} %get-tuple-element.34.refs_1_.refs_0_, bf16[512,512]{1,0:T(8,128)(2,1)} %get-tuple-element.35.refs_1_, bf16[512,512]{1,0:T(8,128)(2,1)} %get-tuple-element.37.refs_2_, ...), custom_call_target="tpu_custom_call" | custom-call | flops 49999998976 | bytes 8 | tf_op jit(solution)/shard_map/project/pallas_call | solution.py:333
  197.4 8.1 %reduce-scatter.6.cloned.1.call-done = bf16[1,2,512,384]{3,2,1,0:T(8,128)(2,1)} async-done(((bf16[4,2,512,384]{3,2,1,0:T(8,128)(2,1)}), bf16[1,2,512,384]{3,2,1,0:T(8,128)(2,1)}) %reduce-scatter.6.cloned.1.call-update) | async-done | bytes 786448 | tf_op jit(solution)/shard_map/reduce_scatter | solution.py:488
  205.5 2.9 %place.8 = (bf16[512,2048]{1,0:T(8,128)(2,1)}, bf16[512,384]{1,0:T(8,128)(2,1)}) custom-call(s32[1]{0:T(128)} %bitcast.side_ref, bf16[2,512,384]{2,1,0:T(8,128)(2,1)} %bitcast.9, bf16[512,2048]{1,0:T(8,128)(2,1)} %place.7.refs_2_.refs_0_), custom_call_target="tpu_custom_call", output_to_operand_aliasing={{0}: (2, {})} | custom-call | flops 200000000 | bytes 8 | tf_op jit(solution)/shard_map/place/pallas_call | solution.py:383
  208.4 1.9 collective-permute-done.18.refs_0_
  210.3 0.8 copy-done.2
  211.1 2.6 place.9.refs_0_
  213.7 54.5 %reduce-scatter.8.cloned.1.call-done = bf16[1,2,512,384]{3,2,1,0:T(8,128)(2,1)} async-done(((bf16[4,2,512,384]{3,2,1,0:T(8,128)(2,1)}), bf16[1,2,512,384]{3,2,1,0:T(8,128)(2,1)}) %reduce-scatter.8.cloned.1.call-update) | async-done | bytes 786448 | tf_op jit(solution)/shard_map/reduce_scatter | solution.py:488
  268.2 2.9 %place.10 = (bf16[512,2048]{1,0:T(8,128)(2,1)}, bf16[512,384]{1,0:T(8,128)(2,1)}) custom-call(s32[1]{0:T(128)} %bitcast.side_ref, bf16[2,512,384]{2,1,0:T(8,128)(2,1)} %bitcast.16, bf16[512,2048]{1,0:T(8,128)(2,1)} %place.9.refs_0_), custom_call_target="tpu_custom_call", output_to_operand_aliasing={{0}: (2, {})} | custom-call | flops 200000000 | bytes 8 | tf_op jit(solution)/shard_map/place/pallas_call | solution.py:383
  271.1 1.9 collective-permute-done.19.refs_0_
  273.0 0.8 copy-done.1
  273.8 2.6 place.11
  (36 shorter events, 3.4 us)
Async XLA Ops:
  6.5 138.3 %reduce-scatter.4.cloned.1.call-start = ((), (), s32[]{:S(2)}) async-start(), calls=%async_computation.3 | async-start | bytes 2621440 | tf_op jit(solution)/shard_map/reduce_scatter | solution.py:488
  7.5 4.0 %collective-permute-start = (bf16[3,2,2048]{2,1,0:T(2,128)(2,1)S(1)}, bf16[3,2,2048]{2,1,0:T(2,128)(2,1)S(1)}, u32[]{:S(2)}, u32[]{:S(2)}) collective-permute-start(bf16[3,2,2048]{2,1,0:T(2,128)(2,1)S(1)} %slice.3), channel_id=1, source_target_pairs={{0,4},{4,8},{8,12},{12,16},{16,20},{20,24},{24,28},{1,5},{5,9},{9,... | collective-permute-start | bytes 73736 | tf_op jit(solution)/shard_map/ppermute | solution.py:28
  11.5 0.6 copy-start.4
  14.1 28.0 %collective-permute-start.1 = (bf16[2048,256]{1,0:T(8,128)(2,1)}, bf16[2048,256]{1,0:T(8,128)(2,1)}, u32[]{:S(2)}, u32[]{:S(2)}) collective-permute-start(bf16[2048,256]{1,0:T(8,128)(2,1)} %cut.2.after_ref), channel_id=1, source_target_pairs={{0,8},{4,12},{8,0},{12,4},{16,24},{20,28},{24,16},{28,20},{1,9},{5... | collective-permute-start | bytes 3145736 | tf_op jit(solution)/shard_map/ppermute | solution.py:23
  18.2 25.1 %collective-permute-start.2 = (bf16[2048,256]{1,0:T(8,128)(2,1)}, bf16[2048,256]{1,0:T(8,128)(2,1)}, u32[]{:S(2)}, u32[]{:S(2)}) collective-permute-start(bf16[2048,256]{1,0:T(8,128)(2,1)} %cut.2.after_ref), channel_id=1, source_target_pairs={{0,16},{4,20},{8,24},{12,28},{16,0},{20,4},{24,8},{28,12},{1,17},{... | collective-permute-start | bytes 3145736 | tf_op jit(solution)/shard_map/ppermute | solution.py:23
  56.4 14.6 %collective-permute-start.3 = (bf16[1024,256]{1,0:T(8,128)(2,1)}, bf16[1024,256]{1,0:T(8,128)(2,1)}, u32[]{:S(2)}, u32[]{:S(2)}) collective-permute-start(bf16[1024,256]{1,0:T(8,128)(2,1)} %get-tuple-element.33.refs_0_), channel_id=1, source_target_pairs={{0,16},{4,20},{8,24},{12,28},{16,0},{20,4},{24,8},{28,12},{1,17},{... | collective-permute-start | bytes 1572872 | tf_op jit(solution)/shard_map/ppermute | solution.py:23
  56.9 14.2 %collective-permute-start.4 = (bf16[1024,256]{1,0:T(8,128)(2,1)}, bf16[1024,256]{1,0:T(8,128)(2,1)}, u32[]{:S(2)}, u32[]{:S(2)}) collective-permute-start(bf16[1024,256]{1,0:T(8,128)(2,1)} %get-tuple-element.36), channel_id=1, source_target_pairs={{0,8},{4,12},{8,0},{12,4},{16,24},{20,28},{24,16},{28,20},{1,9},{5... | collective-permute-start | bytes 1572872 | tf_op jit(solution)/shard_map/ppermute | solution.py:23
  65.4 5.5 %copy-start = (bf16[512,512]{1,0:T(8,128)(2,1)S(1)}, bf16[512,512]{1,0:T(8,128)(2,1)}, u32[]{:S(2)}) copy-start(bf16[512,512]{1,0:T(8,128)(2,1)} %get-tuple-element.35.refs_1_) | copy-start | bytes 1572868
  65.4 13.0 %collective-permute-start.5 = (bf16[512,512]{1,0:T(8,128)(2,1)}, bf16[512,512]{1,0:T(8,128)(2,1)}, u32[]{:S(2)}, u32[]{:S(2)}) collective-permute-start(bf16[512,512]{1,0:T(8,128)(2,1)} %get-tuple-element.34.refs_1_.refs_0_), channel_id=1, source_target_pairs={{0,4},{4,0},{8,12},{12,8},{16,20},{20,16},{24,28},{28,24},{1,5},{5... | collective-permute-start | bytes 1572872 | tf_op jit(solution)/shard_map/ppermute | solution.py:23
  67.7 37.1 %collective-permute-start.10 = (bf16[2048,384]{1,0:T(8,128)(2,1)}, bf16[2048,384]{1,0:T(8,128)(2,1)}, u32[]{:S(2)}, u32[]{:S(2)}) collective-permute-start(bf16[2048,384]{1,0:T(8,128)(2,1)} %cut.3.refs_0_), channel_id=1, source_target_pairs={{0,16},{4,20},{8,24},{12,28},{16,0},{20,4},{24,8},{28,12},{1,17},{... | collective-permute-start | bytes 4718600 | tf_op jit(solution)/shard_map/ppermute | solution.py:23
  68.2 36.8 %collective-permute-start.9 = (bf16[2048,384]{1,0:T(8,128)(2,1)}, bf16[2048,384]{1,0:T(8,128)(2,1)}, u32[]{:S(2)}, u32[]{:S(2)}) collective-permute-start(bf16[2048,384]{1,0:T(8,128)(2,1)} %cut.3.refs_0_), channel_id=1, source_target_pairs={{0,8},{4,12},{8,0},{12,4},{16,24},{20,28},{24,16},{28,20},{1,9},{5... | collective-permute-start | bytes 4718600 | tf_op jit(solution)/shard_map/ppermute | solution.py:23
  70.9 7.6 %collective-permute-start.6 = (bf16[512,512]{1,0:T(8,128)(2,1)S(1)}, bf16[512,512]{1,0:T(8,128)(2,1)}, u32[]{:S(2)}, u32[]{:S(2)}) collective-permute-start(bf16[512,512]{1,0:T(8,128)(2,1)S(1)} %copy-done), channel_id=1, source_target_pairs={{0,4},{4,0},{8,12},{12,8},{16,20},{20,16},{24,28},{28,24},{1,5},{5... | collective-permute-start | bytes 1572872 | tf_op jit(solution)/shard_map/ppermute | solution.py:23
  78.0 2.3 collective-permute-start.7
  78.4 2.6 collective-permute-start.8
  89.8 115.7 %reduce-scatter.6.cloned.1.call-start = ((), (), s32[]{:S(2)}) async-start(), calls=%async_computation.4 | async-start | bytes 3932160 | tf_op jit(solution)/shard_map/reduce_scatter | solution.py:488
  108.4 20.7 %collective-permute-start.13 = (bf16[1024,384]{1,0:T(8,128)(2,1)}, bf16[1024,384]{1,0:T(8,128)(2,1)S(1)}, u32[]{:S(2)}, u32[]{:S(2)}) collective-permute-start(bf16[1024,384]{1,0:T(8,128)(2,1)} %get-tuple-element.41.refs_13_), channel_id=1, source_target_pairs={{0,16},{4,20},{8,24},{12,28},{16,0},{20,4},{24,8},{28,12},{1,17},{... | collective-permute-start | bytes 2359304 | tf_op jit(solution)/shard_map/ppermute | solution.py:23
  110.0 20.8 %collective-permute-start.14 = (bf16[1024,384]{1,0:T(8,128)(2,1)}, bf16[1024,384]{1,0:T(8,128)(2,1)}, u32[]{:S(2)}, u32[]{:S(2)}) collective-permute-start(bf16[1024,384]{1,0:T(8,128)(2,1)} %get-tuple-element.42), channel_id=1, source_target_pairs={{0,8},{4,12},{8,0},{12,4},{16,24},{20,28},{24,16},{28,20},{1,9},{5... | collective-permute-start | bytes 2359304 | tf_op jit(solution)/shard_map/ppermute | solution.py:23
  110.3 52.2 %collective-permute-start.11 = (bf16[2048,384]{1,0:T(8,128)(2,1)}, bf16[2048,384]{1,0:T(8,128)(2,1)}, u32[]{:S(2)}, u32[]{:S(2)}) collective-permute-start(bf16[2048,384]{1,0:T(8,128)(2,1)} %get-tuple-element.40), channel_id=1, source_target_pairs={{0,8},{4,12},{8,0},{12,4},{16,24},{20,28},{24,16},{28,20},{1,9},{5... | collective-permute-start | bytes 4718600 | tf_op jit(solution)/shard_map/ppermute | solution.py:23
  112.1 50.5 %collective-permute-start.12 = (bf16[2048,384]{1,0:T(8,128)(2,1)}, bf16[2048,384]{1,0:T(8,128)(2,1)}, u32[]{:S(2)}, u32[]{:S(2)}) collective-permute-start(bf16[2048,384]{1,0:T(8,128)(2,1)} %get-tuple-element.40), channel_id=1, source_target_pairs={{0,16},{4,20},{8,24},{12,28},{16,0},{20,4},{24,8},{28,12},{1,17},{... | collective-permute-start | bytes 4718600 | tf_op jit(solution)/shard_map/ppermute | solution.py:23
  129.1 1.7 copy-start.5
  144.9 123.3 %reduce-scatter.8.cloned.1.call-start = ((), (), s32[]{:S(2)}) async-start(), calls=%async_computation.5 | async-start | bytes 3932160 | tf_op jit(solution)/shard_map/reduce_scatter | solution.py:488
  164.9 18.0 %collective-permute-start.15 = (bf16[1024,384]{1,0:T(8,128)(2,1)}, bf16[1024,384]{1,0:T(8,128)(2,1)}, u32[]{:S(2)}, u32[]{:S(2)}) collective-permute-start(bf16[1024,384]{1,0:T(8,128)(2,1)} %get-tuple-element.45.refs_13_), channel_id=1, source_target_pairs={{0,16},{4,20},{8,24},{12,28},{16,0},{20,4},{24,8},{28,12},{1,17},{... | collective-permute-start | bytes 2359304 | tf_op jit(solution)/shard_map/ppermute | solution.py:23
  165.6 17.8 %collective-permute-start.16 = (bf16[1024,384]{1,0:T(8,128)(2,1)}, bf16[1024,384]{1,0:T(8,128)(2,1)}, u32[]{:S(2)}, u32[]{:S(2)}) collective-permute-start(bf16[1024,384]{1,0:T(8,128)(2,1)} %get-tuple-element.46), channel_id=1, source_target_pairs={{0,8},{4,12},{8,0},{12,4},{16,24},{20,28},{24,16},{28,20},{1,9},{5... | collective-permute-start | bytes 2359304 | tf_op jit(solution)/shard_map/ppermute | solution.py:23
  168.8 1.7 collective-permute-start.17
  170.5 0.7 copy-start.3
  208.4 1.9 collective-permute-start.18
  210.3 0.8 copy-start.2
  271.1 1.9 collective-permute-start.19
  273.0 0.8 copy-start.1
Sparse Core Ops, SparseCore 0:
  89.9 44.2 reduce-scatter.3
  145.0 60.4 reduce-scatter.5
  207.9 60.2 reduce-scatter.7

commit v2 on v1

--- a/solution.py
+++ b/solution.py
@@ -9,10 +9,15 @@
 
 F32 = jnp.float32
 BF16 = jnp.bfloat16
+STEPS = 2
 TILES = 4
+REACHES = (1, 2, 4)
 SUB = 8
 LANES = 128
 CUTS = 4
+K1COST = 60
+MIXCOST = 20
+PA, PB, PC = 0.1, 35, 50
 VMEM = 63 * 1024 * 1024
 SMEM_SPEC = pl.BlockSpec(memory_space=pltpu.SMEM)
 ANY_SPEC = pl.BlockSpec(memory_space=pl.ANY)
@@ -55,7 +60,7 @@
 
 
 def local_kernel(
-    k_ref, v_ref, halo_ref, taps_ref, rates_ref, coef_ref, bias_ref, after_ref,
+    k_ref, v_ref, halo_ref, taps_ref, rates_ref, residues_ref, bias_ref, after_ref,
     y_ref, entry_ref, end_ref, k_rows, v_rows, ends,
 ):
     rows, width = k_ref.shape[1], k_ref.shape[2]
@@ -70,8 +75,11 @@
         v_rows[pl.ds(SUB - 2, 2), :] = halo_ref[2, :, lanes].astype(F32)
         k_rows[pl.ds(SUB, rows), :] = k_ref[0, :, lanes].astype(F32)
         v_rows[pl.ds(SUB, rows), :] = v_ref[0, :, lanes].astype(F32)
-        decay = [spread(jnp.exp(-rates_ref[m : m + 1, lanes])) for m in range(order)]
-        coef = [spread(coef_ref[m : m + 1, lanes]) for m in range(order)]
+        rates = rates_ref[:, lanes]
+        all_decay = jnp.exp(-rates)
+        all_coef = residues_ref[:, lanes] * jnp.sqrt(2.0 * rates)
+        decay = [spread(all_decay[m : m + 1, :]) for m in range(order)]
+        coef = [spread(all_coef[m : m + 1, :]) for m in range(order)]
         bias = spread(bias_ref[0:1, lanes])
         kt = [spread(taps_ref[1, j : j + 1, lanes]) for j in range(3)]
         vt = [spread(taps_ref[2, j : j + 1, lanes]) for j in range(3)]
@@ -95,14 +103,12 @@
         zero = jnp.zeros((SUB, LANES), F32)
         start = (pick(k_rows, -1), pick(k_rows, -2), pick(v_rows, -1), pick(v_rows, -2), [zero] * order)
         state = lax.fori_loop(0, length // unroll, steps, start)[4]
+        leaps = {reach: jnp.exp(rates * float(-length * reach)) for reach in REACHES}
         for m in range(order):
-            rate = spread(rates_ref[m : m + 1, lanes])
             scan = state[m]
-            reach = 1
-            while reach < SUB:
-                earlier = pltpu.roll(scan, reach, 0) * jnp.exp(-rate * float(length * reach))
+            for reach in REACHES:
+                earlier = pltpu.roll(scan, reach, 0) * spread(leaps[reach][m : m + 1, :])
                 scan = scan + jnp.where(sub >= reach, earlier, 0.0)
-                reach *= 2
             entry_ref[m, :, lanes] = jnp.where(sub >= 1, pltpu.roll(scan, 1, 0), 0.0)
             ends[m : m + 1, :] = scan[SUB - 1 :, :]
         end_ref[:, lanes] = ends[...].astype(end_ref.dtype)
@@ -111,7 +117,7 @@
     lax.fori_loop(0, width // LANES, group, 0)
 
 
-def local_part(projected, halo, taps, rates, coef, bias, after):
+def local_part(projected, halo, taps, rates, residues, bias, after):
     rows, width = projected.shape[1:]
     order = rates.shape[0]
     tile = width // TILES
@@ -145,20 +151,22 @@
             pltpu.VMEM((order, LANES), F32),
         ],
         compiler_params=params(),
-        cost_estimate=cost(20, 12 * rows * width),
+        cost_estimate=cost(K1COST, 12 * rows * width),
         name="local_conv",
-    )(projected, projected, halo, taps, rates, coef, bias, after)
+    )(projected, projected, halo, taps, rates, residues, bias, after)
 
 
 def mix_kernel(
-    count, mine_ref, q_ref, halo_ref, taps_ref, rates_ref, y_ref, entry_ref, ends_ref, *refs
+    count, cut, mine_ref, q_ref, halo_ref, taps_ref, rates_ref, y_ref, entry_ref, ends_ref, *refs
 ):
-    outs, (q_rows, mixed_rows) = refs[-2 - count : -2], refs[-2:]
+    outs, (q_rows, mixed_rows) = refs[-2 - count - cut : -2 - cut], refs[-2:]
+    if cut:
+        refs[-3][...] = refs[0][...]
     rows, width = q_ref.shape[1], q_ref.shape[2]
     order = rates_ref.shape[0]
     length = rows // SUB
     unroll = min(8, length)
-    sub = lax.broadcasted_iota(jnp.int32, (SUB, LANES), 0).astype(F32)
+    sub = lax.broadcasted_iota(jnp.int32, (SUB, LANES), 0)
 
     def group(index, _):
         lanes = pl.ds(pl.multiple_of(index * LANES, LANES), LANES)
@@ -171,13 +179,14 @@
         q_rows[pl.ds(SUB - 2, 2), :] = halo_ref[0, :, lanes].astype(F32)
         q_rows[pl.ds(SUB, rows), :] = q_ref[0, :, lanes].astype(F32)
         decay, carried = [], []
+        all_decay = jnp.exp(-rates)
+        leaps = {reach: jnp.exp(rates * float(-length * reach)) for reach in REACHES}
         for m in range(order):
-            rate = spread(rates[m : m + 1, :])
-            decay.append(jnp.exp(-rate))
-            at_entry = entry_ref[m, :, lanes] + spread(before[m : m + 1, :]) * jnp.exp(
-                -rate * (sub * float(length))
-            )
-            carried.append(at_entry * decay[m])
+            decay.append(spread(all_decay[m : m + 1, :]))
+            passed = spread(before[m : m + 1, :])
+            for reach in REACHES:
+                passed = jnp.where(sub & reach == 0, passed, passed * spread(leaps[reach][m : m + 1, :]))
+            carried.append((entry_ref[m, :, lanes] + passed) * decay[m])
         qt = [spread(taps_ref[0, j : j + 1, lanes]) for j in range(3)]
 
         def pick(b):
@@ -207,35 +216,51 @@
     lax.fori_loop(0, width // LANES, group, 0)
 
 
-def mix_part(mine, projected, halo, taps, rates, y, entry, ends, tiles, after):
+def mix_part(mine, projected, halo, taps, rates, y, entry, ends, tiles, cut, after):
     rows, width = projected.shape[1:]
     order = rates.shape[0]
     tile = width // TILES
     length = rows // SUB
     first, count = tiles[0], len(tiles)
+    in_specs = [
+        SMEM_SPEC,
+        pl.BlockSpec((1, rows, tile), lambda c: (0, 0, first + c)),
+        pl.BlockSpec((3, 2, tile), lambda c: (0, 0, first + c)),
+        pl.BlockSpec((3, 3, tile), lambda c: (0, 0, first + c)),
+        pl.BlockSpec((order, tile), lambda c: (0, first + c)),
+        pl.BlockSpec((length, SUB, tile), lambda c: (0, 0, first + c)),
+        pl.BlockSpec((order, SUB, tile), lambda c: (0, 0, first + c)),
+        pl.BlockSpec((ends.shape[0], order, tile), lambda c: (0, 0, first + c)),
+    ]
+    out_specs = [pl.BlockSpec((rows, tile), lambda c: (0, 0))] * count
+    out_shape = [jax.ShapeDtypeStruct((rows, tile), BF16)] * count
+    args = [mine, projected, halo, taps, rates, y, entry, ends]
+    if cut:
+        w, column, columns = cut
+        depth = w.shape[0] // STEPS
+        in_specs.append(
+            pl.BlockSpec(
+                (pl.Element(depth), pl.Element(columns)),
+                lambda c: (jnp.minimum(c, STEPS - 1) * depth, column),
+            )
+        )
+        out_specs.append(pl.BlockSpec((depth, columns), lambda c: (jnp.minimum(c, STEPS - 1), 0)))
+        out_shape.append(jax.ShapeDtypeStruct((w.shape[0], columns), BF16))
+        args.append(w)
     return pl.pallas_call(
-        functools.partial(mix_kernel, count),
+        functools.partial(mix_kernel, count, cut is not None),
         grid=(count,),
-        in_specs=[
-            SMEM_SPEC,
-            pl.BlockSpec((1, rows, tile), lambda c: (0, 0, first + c)),
-            pl.BlockSpec((3, 2, tile), lambda c: (0, 0, first + c)),
-            pl.BlockSpec((3, 3, tile), lambda c: (0, 0, first + c)),
-            pl.BlockSpec((order, tile), lambda c: (0, first + c)),
-            pl.BlockSpec((length, SUB, tile), lambda c: (0, 0, first + c)),
-            pl.BlockSpec((order, SUB, tile), lambda c: (0, 0, first + c)),
-            pl.BlockSpec((ends.shape[0], order, tile), lambda c: (0, 0, first + c)),
-        ] + [ANY_SPEC] * len(after),
-        out_specs=[pl.BlockSpec((rows, tile), lambda c: (0, 0))] * count,
-        out_shape=[jax.ShapeDtypeStruct((rows, tile), BF16)] * count,
+        in_specs=in_specs + [ANY_SPEC] * len(after),
+        out_specs=out_specs,
+        out_shape=out_shape,
         scratch_shapes=[
             pltpu.VMEM((rows + SUB, LANES), F32),
             pltpu.VMEM((rows, LANES), F32),
         ],
         compiler_params=params(),
-        cost_estimate=cost(20, 8),
+        cost_estimate=cost(MIXCOST, 8),
         name="mix",
-    )(mine, projected, halo, taps, rates, y, entry, ends, *after)
+    )(*args, *after)
 
 
 def join_kernel(*refs):
@@ -293,13 +318,13 @@
     )(*arrays, *after)
 
 
-def project_kernel(parts, slot_ref, *refs):
+def project_kernel(first, parts, slot_ref, *refs):
     sides = [
         jnp.concatenate([ref[...] for ref in refs[side * TILES : (side + 1) * TILES]], axis=1)
         for side in range(2)
     ]
     refs = refs[2 * TILES :]
-    weights, (after_ref, out_ref, token_ref) = refs[: sum(parts)], refs[sum(parts) :]
+    weights, (out_ref, token_ref) = refs[: sum(parts)], refs[-2:]
     token_ref[...] = jnp.zeros(token_ref.shape, F32)
     at = 0
     for piece, count in enumerate(parts):
@@ -311,41 +336,55 @@
                 term = jnp.dot(tokens[:, low : low + depth], part[...], preferred_element_type=F32)
                 result = term if result is None else result + term
                 low += depth
-            out_ref[piece ^ slot_ref[0], side] = result.astype(BF16)
+            out_ref[piece ^ slot_ref[0] if first else 0, side] = result.astype(BF16)
         at += count
 
 
-def project_part(slot, own, other, pieces, first, width, weight, after):
+def project_part(slot, own, other, pieces, column, width, weight, out, count, after):
     rows, depth = own[0].shape
     parts = [len(piece) for piece in pieces]
     weights = [part for piece in pieces for part in piece]
     steps = 2
     tile = rows // steps
-    in_specs = [SMEM_SPEC] + [pl.BlockSpec((tile, depth), lambda i: (i, 0))] * (2 * TILES)
+    in_specs = [pl.BlockSpec((tile, depth), lambda i, slot_ref: (i, 0))] * (2 * TILES)
     for i, part in enumerate(weights):
-        if i == 0:
+        if i == 0 and out is None:
             in_specs.append(
-                pl.BlockSpec((pl.Element(part.shape[0]), pl.Element(width)), lambda i: (0, first))
+                pl.BlockSpec(
+                    (pl.Element(part.shape[0]), pl.Element(width)), lambda i, slot_ref: (0, column)
+                )
             )
         else:
-            in_specs.append(pl.BlockSpec(part.shape, lambda i: (0, 0)))
-    count = len(pieces)
+            in_specs.append(pl.BlockSpec(part.shape, lambda i, slot_ref: (0, 0)))
+    args = [*own, *other, *weights, *after]
+    in_specs += [ANY_SPEC] * len(after)
+    aliases = {}
+    if out is None:
+        out_spec = pl.BlockSpec((count, 2, tile, width), lambda i, slot_ref: (0, 0, i, 0))
+    else:
+        out_spec = pl.BlockSpec(
+            (1, 2, tile, width), lambda i, slot_ref: ((count - 1) ^ slot_ref[0], 0, i, 0)
+        )
+        aliases = {1 + len(args): 0}
+        in_specs.append(ANY_SPEC)
+        args.append(out)
     return pl.pallas_call(
-        functools.partial(project_kernel, parts),
-        grid=(steps,),
-        in_specs=in_specs + [ANY_SPEC],
-        out_specs=[
-            pl.BlockSpec((count, 2, tile, width), lambda i: (0, 0, i, 0)),
-            pl.BlockSpec((SUB, LANES), lambda i: (0, 0)),
-        ],
+        functools.partial(project_kernel, out is None, parts),
+        grid_spec=pltpu.PrefetchScalarGridSpec(
+            num_scalar_prefetch=1,
+            grid=(steps,),
+            in_specs=in_specs,
+            out_specs=[out_spec, pl.BlockSpec((SUB, LANES), lambda i, slot_ref: (0, 0))],
+        ),
         out_shape=[
             jax.ShapeDtypeStruct((count, 2, rows, width), BF16),
             jax.ShapeDtypeStruct((SUB, LANES), F32),
         ],
+        input_output_aliases=aliases,
         compiler_params=params(),
         cost_estimate=cost(weight, 8),
         name="project",
-    )(slot, *own, *other, *weights, after)
+    )(slot, *args)
 
 
 def place_kernel(side_ref, *refs):
@@ -405,7 +444,6 @@
     assert per == 2
     mine = lax.axis_index("ctx")
     slot = ((mine // per) ^ lax.axis_index("ch")).astype(jnp.int32)[None]
-    coef = residues * jnp.sqrt(2.0 * rates)
     near, far = 2, 4
     more = [1 << b for b in range(3, 16) if 1 << b < count]
 
@@ -445,23 +483,24 @@
                 pieces[r ^ mask] = [swap(part, "ctx", mask) for part in parts]
         return [pieces[r] for r in sorted(pieces)]
 
-    halo = from_behind(projected[:, rows - 2 :, :], "ctx")
-    (sent,) = copy_part([cut_of(0)], [halo], "cut")
+    last = projected[:, rows - 2 :, :]
+    halo = from_behind(last, "ctx")
+    (sent,) = copy_part([cut_of(0)], [last], "cut")
     arrived = first_hops(sent)
-    y, entry, end = local_part(projected, halo, short_weight, rates, coef, bias[None], sent)
+    y, entry, end = local_part(projected, halo, short_weight, rates, residues, bias[None], sent)
     ends = lax.all_gather(join_part(end, arrived), "ctx")
     token, diagonal, _ = second_hops(0, arrived, [ends], then=False)
-    mixed, other = [], []
-    for tiles in (range(TILES // 2), range(TILES // 2, TILES)):
-        made = mix_part(
-            mine.astype(jnp.int32)[None], projected, halo, short_weight, rates, y, entry, ends, tiles,
-            [token, *(diagonal if mixed else ())],
-        )
-        if not mixed:
-            (token,) = copy_part([cut_of(1)], [made[0]], "cut")
-            upcoming = first_hops(token)
-        mixed += made
-        other += [swap(part, "ctx", 1) for part in made]
+    early = TILES - 1
+    *mixed, sent = mix_part(
+        mine.astype(jnp.int32)[None], projected, halo, short_weight, rates, y, entry, ends,
+        range(early), (out_weight, starts[1], widths[1]), [token],
+    )
+    upcoming = first_hops(sent)
+    mixed += mix_part(
+        mine.astype(jnp.int32)[None], projected, halo, short_weight, rates, y, entry, ends,
+        range(early, TILES), None, [sent, *diagonal],
+    )
+    other = [swap(part, "ctx", 1) for part in mixed]
     token = mixed[-1]
     slot = (mine // per).astype(jnp.int32)[None]
     side = (mine % per).astype(jnp.int32)[None]
@@ -477,9 +516,18 @@
             arrived = upcoming
             token, diagonal, upcoming = second_hops(s, arrived, [token, *sums[: s - 1]])
         pieces = pieces_of(s, arrived, diagonal)
-        partial, token = project_part(
-            slot, mixed, other, pieces, starts[s], widths[s], (0.1, 35, 50)[s], token
-        )
+        weight = (PA, PB, PC)[s]
+        if s == 0:
+            partial, token = project_part(
+                slot, mixed, other, pieces, starts[s], widths[s], weight, None, groups, [token]
+            )
+        else:
+            partial, token = project_part(
+                slot, mixed, other, pieces[:-1], starts[s], widths[s], 0.1, None, groups, [token]
+            )
+            partial, token = project_part(
+                slot, mixed, other, pieces[-1:], starts[s], widths[s], weight, partial, groups, [token]
+            )
         if s == stages - 1:
             out = place_stage(0, None)
             partial = join_part(partial, [sums[-1], out])

time: 284 us -> 272 us (0.958)
  waiting for transfers between devices: 137 us -> 124 us
  Pallas kernels: 97.2 us -> 102 us
    ppermute x19, waiting for transfers between devices: 74.2 us -> 60.5 us  [swap(): return lax.ppermute(value, axis, [(i, i ^ mask) for i in range(count)])]
    pallas_call x5 -> x7, Pallas kernels: 50.7 us -> 57.7 us  [the longest x5 42.9 us: project_part(): pl.pallas_call(functools.partial(project_kernel, out is None, parts), gri...]
    pallas_call x5 -> x4, Pallas kernels: 12.1 us -> 9.7 us  [copy_part(): pl.pallas_call(functools.partial(copy_kernel, places), in_specs=[ANY_SPEC...]
  transfers between devices with their start and end apart: 23 -> 23, of which waited for: 18 -> 15; matrix products, arithmetic and copies ran while one was open for 1% -> 0% of each run, Pallas kernels for 31% -> 35%
where the time goes in v2:
time: 272 us
  waiting for transfers between devices  124 us (46%)
  Pallas kernels  102 us (38%)
  starting transfers between devices  17.9 us (7%)
  between operations  13.2 us (5%)
  blocking collectives  10.8 us (4%)
  local copies, waits for them, and re-layouts  3.75 us (1%)
    reduce_scatter x3, waiting for transfers between devices, body(): sums.append(lax.psum_scatter(partial, 'ch', scatter_dimension=0))  63.7 us
    ppermute x19, waiting for transfers between devices, swap(): return lax.ppermute(value, axis, [(i, i ^ mask) for i in range(count)])  60.5 us
    pallas_call x5, Pallas kernels, project_part(): pl.pallas_call(functools.partial(project_kernel, out is None, parts), gri...  42.9 us
    pallas_call x1, Pallas kernels, local_part(): pl.pallas_call(local_kernel, grid=(width // tile,), in_specs=[pl.BlockSpe...  19.9 us
    ppermute x19, starting transfers between devices, swap(): return lax.ppermute(value, axis, [(i, i ^ mask) for i in range(count)])  15.3 us
    pallas_call x2, Pallas kernels, mix_part(): pl.pallas_call(functools.partial(mix_kernel, count, cut is not None), gri...  14.8 us
    pallas_call x6, Pallas kernels, place_part(): pl.pallas_call(place_both_kernel if landed is None else place_kernel, gri...  14.4 us
    all_gather x1, blocking collectives, body(): ends = lax.all_gather(join_part(end, arrived), 'ctx')  10.8 us
  transfers between devices with their start and end apart: 23, of which 15 were waited for; matrix products, arithmetic and copies ran while one was open for 0% of the time, Pallas kernels for 35%

profile of v2, /device:TPU:0, one launch (start us, length us, event | category | flops | bytes accessed | tf_op | source)
XLA Modules:
  0.0 271.8 jit_solution(4157629601270492129)
XLA Ops:
  6.5 0.9 slice.3.refs_1_
  7.5 2.4 collective-permute-start
  9.8 2.0 cut.1.after_ref
  11.8 2.6 collective-permute-start.1
  14.4 1.5 collective-permute-start.2
  16.5 19.9 %local_conv.1 = (f32[64,8,2048]{2,1,0:T(8,128)}, f32[16,8,2048]{2,1,0:T(8,128)}, bf16[16,2048]{1,0:T(8,128)(2,1)}) custom-call(bf16[3,512,2048]{2,1,0:T(8,128)(2,1)} %q_ref.3, bf16[3,512,2048]{2,1,0:T(8,128)(2,1)} %q_ref.3, bf16[3,2,2048]{2,1,0:T(2,128)(2,1)} %copy-done.6, f32[3,3,2048]{2,1,0:T(4,128)} %taps_ref.5, f32[16,2048]{1,0:T(8,128)} %rates_ref.5, ...), custom_call_target="tpu_custom_call" | custom-call | flops 60000002048 | bytes 12582912 | tf_op jit(solution)/shard_map/local_conv/pallas_call | solution.py:125
  36.5 1.2 collective-permute-done.1.refs_1_.refs_0_.refs_9_
  37.7 2.7 collective-permute-done.2.refs_2_.refs_1_.refs_10_
  40.4 10.8 %all-gather = bf16[128,2048]{1,0:T(8,128)(2,1)} all-gather(bf16[16,2048]{1,0:T(8,128)(2,1)} %join.3), channel_id=2, replica_groups=mesh['ctx'=8,'ch'=4] {'ctx'}, dimensions={0}, use_global_device_ids=true | all-gather | bytes 589824 | tf_op jit(solution)/shard_map/all_gather | solution.py:491
  51.2 2.1 pass_weights.3
  53.3 1.1 collective-permute-start.3
  54.4 1.0 collective-permute-start.4
  55.4 10.3 %mix.2 = (bf16[512,512]{1,0:T(8,128)(2,1)}, bf16[512,512]{1,0:T(8,128)(2,1)}, bf16[512,512]{1,0:T(8,128)(2,1)}, bf16[2048,384]{1,0:T(8,128)(2,1)}) custom-call(s32[1]{0:T(128)} %bitcast.2.mine_ref, bf16[3,512,2048]{2,1,0:T(8,128)(2,1)} %q_ref.3, bf16[3,2,2048]{2,1,0:T(2,128)(2,1)} %copy-done.6, f32[3,3,2048]{2,1,0:T(4,128)} %taps_ref.5, ...), custom_call_target="tpu_custom_call" | custom-call | flops 20000000000 | bytes 8 | tf_op jit(solution)/shard_map/mix/pallas_call | solution.py:250
  65.7 1.0 collective-permute-start.10
  66.7 1.0 collective-permute-start.9
  68.6 4.5 %mix.3.refs_3_.refs_13_ = bf16[512,512]{1,0:T(8,128)(2,1)} custom-call(s32[1]{0:T(128)} %bitcast.2.mine_ref, bf16[3,512,2048]{2,1,0:T(8,128)(2,1)} %q_ref.3, bf16[3,2,2048]{2,1,0:T(2,128)(2,1)} %copy-done.6, f32[3,3,2048]{2,1,0:T(4,128)} %taps_ref.5, f32[16,2048]{1,0:T(8,128)} %rates_ref.5, f32[64,8,2048]{2,1,0:T(8,128)} %get-tuple-element.34.y_ref, ...), custom_call_target="tpu_custom_call" | custom-call | flops 20000000000 | bytes 8 | tf_op jit(solution)/shard_map/mix/pallas_call | solution.py:250
  73.7 1.9 collective-permute-done.8.refs_7_
  75.5 8.7 %project.5 = (bf16[4,2,512,256]{3,2,1,0:T(8,128)(2,1)}, f32[8,128]{1,0:T(8,128)}) custom-call(s32[1]{0:T(128)} %bitcast.1.slot_ref, bf16[512,512]{1,0:T(8,128)(2,1)} %get-tuple-element.38.refs_0_, bf16[512,512]{1,0:T(8,128)(2,1)} %get-tuple-element.39.refs_1_, bf16[512,512]{1,0:T(8,128)(2,1)} %get-tuple-element.40.refs_2_, ...), custom_call_target="tpu_custom_call" | custom-call | flops 100000000 | bytes 8 | tf_op jit(solution)/shard_map/project/pallas_call | solution.py:371
  84.4 17.8 %collective-permute-done.10.refs_1_.refs_10_ = bf16[2048,384]{1,0:T(8,128)(2,1)} collective-permute-done((bf16[2048,384]{1,0:T(8,128)(2,1)}, bf16[2048,384]{1,0:T(8,128)(2,1)}, u32[]{:S(2)}, u32[]{:S(2)}) %collective-permute-start.10) | collective-permute-done | bytes 1572896 | tf_op jit(solution)/shard_map/ppermute | solution.py:28
  102.1 0.8 collective-permute-done.9.refs_0_.refs_9_
  102.9 3.3 %pass_weights.4 = (bf16[1024,384]{1,0:T(8,128)(2,1)}, bf16[1024,384]{1,0:T(8,128)(2,1)}, bf16[2048,384]{1,0:T(8,128)(2,1)}) custom-call(bf16[2048,384]{1,0:T(8,128)(2,1)} %collective-permute-done.9.refs_0_.refs_9_, bf16[2048,384]{1,0:T(8,128)(2,1)} %collective-permute-done.10.refs_1_.refs_10_, bf16[2048,1024]{1,0:T(8,128)(2,1)} %refs_8_.5, ...), custom_call_target="tpu_custom_call" | custom-call | flops 100000000 | bytes 8 | tf_op jit(solution)/shard_map/pass_weights/pallas_call | solution.py:308
  106.1 1.2 collective-permute-start.13
  107.3 1.1 collective-permute-start.14
  108.4 1.0 collective-permute-start.11
  109.3 0.9 collective-permute-start.12
  110.3 11.4 %project.6 = (bf16[4,2,512,384]{3,2,1,0:T(8,128)(2,1)}, f32[8,128]{1,0:T(8,128)}) custom-call(s32[1]{0:T(128)} %bitcast.1.slot_ref, bf16[512,512]{1,0:T(8,128)(2,1)} %get-tuple-element.38.refs_0_, bf16[512,512]{1,0:T(8,128)(2,1)} %get-tuple-element.39.refs_1_, bf16[512,512]{1,0:T(8,128)(2,1)} %get-tuple-element.40.refs_2_, ...), custom_call_target="tpu_custom_call" | custom-call | flops 100000000 | bytes 8 | tf_op jit(solution)/shard_map/project/pallas_call | solution.py:371
  121.7 5.2 %collective-permute-done.13.refs_8_ = bf16[1024,384]{1,0:T(8,128)(2,1)S(1)} collective-permute-done((bf16[1024,384]{1,0:T(8,128)(2,1)}, bf16[1024,384]{1,0:T(8,128)(2,1)S(1)}, u32[]{:S(2)}, u32[]{:S(2)}) %collective-permute-start.13) | collective-permute-done | bytes 786464 | tf_op jit(solution)/shard_map/ppermute | solution.py:28
  126.9 1.2 collective-permute-done.14.refs_9_
  128.1 5.6 %project.7 = (bf16[4,2,512,384]{3,2,1,0:T(8,128)(2,1)}, f32[8,128]{1,0:T(8,128)}) custom-call(s32[1]{0:T(128)} %bitcast.1.slot_ref, bf16[512,512]{1,0:T(8,128)(2,1)} %get-tuple-element.38.refs_0_, bf16[512,512]{1,0:T(8,128)(2,1)} %get-tuple-element.39.refs_1_, bf16[512,512]{1,0:T(8,128)(2,1)} %get-tuple-element.40.refs_2_, ...), custom_call_target="tpu_custom_call", output_to_operand_aliasing={{0}: (12, {})} | custom-call | flops 35000000512 | bytes 8 | tf_op jit(solution)/shard_map/project/pallas_call | solution.py:371
  134.0 25.0 %collective-permute-done.11.refs_0_.refs_9_ = bf16[2048,384]{1,0:T(8,128)(2,1)} collective-permute-done((bf16[2048,384]{1,0:T(8,128)(2,1)}, bf16[2048,384]{1,0:T(8,128)(2,1)}, u32[]{:S(2)}, u32[]{:S(2)}) %collective-permute-start.11) | collective-permute-done | bytes 1572896 | tf_op jit(solution)/shard_map/ppermute | solution.py:28
  159.0 2.4 pass_weights.5
  161.3 1.2 collective-permute-start.15
  162.6 0.9 collective-permute-start.16
  163.4 1.8 place.6
  165.2 11.5 %project.8 = (bf16[4,2,512,384]{3,2,1,0:T(8,128)(2,1)}, f32[8,128]{1,0:T(8,128)}) custom-call(s32[1]{0:T(128)} %bitcast.1.slot_ref, bf16[512,512]{1,0:T(8,128)(2,1)} %get-tuple-element.38.refs_0_, bf16[512,512]{1,0:T(8,128)(2,1)} %get-tuple-element.39.refs_1_, bf16[512,512]{1,0:T(8,128)(2,1)} %get-tuple-element.40.refs_2_, ...), custom_call_target="tpu_custom_call" | custom-call | flops 100000000 | bytes 8 | tf_op jit(solution)/shard_map/project/pallas_call | solution.py:371
  176.8 0.7 copy-done.3
  177.4 1.6 place.7.refs_2_.refs_0_
  179.5 5.6 %project.9 = (bf16[4,2,512,384]{3,2,1,0:T(8,128)(2,1)}, f32[8,128]{1,0:T(8,128)}) custom-call(s32[1]{0:T(128)} %bitcast.1.slot_ref, bf16[512,512]{1,0:T(8,128)(2,1)} %get-tuple-element.38.refs_0_, bf16[512,512]{1,0:T(8,128)(2,1)} %get-tuple-element.39.refs_1_, bf16[512,512]{1,0:T(8,128)(2,1)} %get-tuple-element.40.refs_2_, ...), custom_call_target="tpu_custom_call", output_to_operand_aliasing={{0}: (12, {})} | custom-call | flops 49999998976 | bytes 8 | tf_op jit(solution)/shard_map/project/pallas_call | solution.py:371
  185.1 9.2 %reduce-scatter.6.cloned.1.call-done = bf16[1,2,512,384]{3,2,1,0:T(8,128)(2,1)} async-done(((bf16[4,2,512,384]{3,2,1,0:T(8,128)(2,1)}), bf16[1,2,512,384]{3,2,1,0:T(8,128)(2,1)}) %reduce-scatter.6.cloned.1.call-update) | async-done | bytes 786448 | tf_op jit(solution)/shard_map/reduce_scatter | solution.py:536
  194.3 2.9 %place.8 = (bf16[512,2048]{1,0:T(8,128)(2,1)}, bf16[512,384]{1,0:T(8,128)(2,1)}) custom-call(s32[1]{0:T(128)} %bitcast.side_ref, bf16[2,512,384]{2,1,0:T(8,128)(2,1)} %bitcast.9, bf16[512,2048]{1,0:T(8,128)(2,1)} %place.7.refs_2_.refs_0_), custom_call_target="tpu_custom_call", output_to_operand_aliasing={{0}: (2, {})} | custom-call | flops 200000000 | bytes 8 | tf_op jit(solution)/shard_map/place/pallas_call | solution.py:422
  197.2 1.9 collective-permute-done.18.refs_0_
  199.2 0.8 copy-done.2
  199.9 2.6 place.9.refs_0_
  202.6 54.5 %reduce-scatter.8.cloned.1.call-done = bf16[1,2,512,384]{3,2,1,0:T(8,128)(2,1)} async-done(((bf16[4,2,512,384]{3,2,1,0:T(8,128)(2,1)}), bf16[1,2,512,384]{3,2,1,0:T(8,128)(2,1)}) %reduce-scatter.8.cloned.1.call-update) | async-done | bytes 786448 | tf_op jit(solution)/shard_map/reduce_scatter | solution.py:536
  257.1 2.9 %place.10 = (bf16[512,2048]{1,0:T(8,128)(2,1)}, bf16[512,384]{1,0:T(8,128)(2,1)}) custom-call(s32[1]{0:T(128)} %bitcast.side_ref, bf16[2,512,384]{2,1,0:T(8,128)(2,1)} %bitcast.16, bf16[512,2048]{1,0:T(8,128)(2,1)} %place.9.refs_0_), custom_call_target="tpu_custom_call", output_to_operand_aliasing={{0}: (2, {})} | custom-call | flops 200000000 | bytes 8 | tf_op jit(solution)/shard_map/place/pallas_call | solution.py:422
  259.9 1.9 collective-permute-done.19.refs_0_
  261.9 0.7 copy-done.1
  262.6 2.6 place.11
  (38 shorter events, 2.8 us)
Async XLA Ops:
  6.5 127.2 %reduce-scatter.4.cloned.1.call-start = ((), (), s32[]{:S(2)}) async-start(), calls=%async_computation.3 | async-start | bytes 2621440 | tf_op jit(solution)/shard_map/reduce_scatter | solution.py:536
  7.5 2.4 copy-start.4
  7.5 8.5 %collective-permute-start = (bf16[3,2,2048]{2,1,0:T(2,128)(2,1)S(1)}, bf16[3,2,2048]{2,1,0:T(2,128)(2,1)S(1)}, u32[]{:S(2)}, u32[]{:S(2)}) collective-permute-start(bf16[3,2,2048]{2,1,0:T(2,128)(2,1)S(1)} %slice.3.refs_1_), channel_id=1, source_target_pairs={{0,4},{4,8},{8,12},{12,16},{16,20},{20,24},{24,28},{1,5},{5,9},{9,... | collective-permute-start | bytes 73736 | tf_op jit(solution)/shard_map/ppermute | solution.py:33
  11.8 25.9 %collective-permute-start.1 = (bf16[2048,256]{1,0:T(8,128)(2,1)}, bf16[2048,256]{1,0:T(8,128)(2,1)}, u32[]{:S(2)}, u32[]{:S(2)}) collective-permute-start(bf16[2048,256]{1,0:T(8,128)(2,1)} %cut.1.after_ref), channel_id=1, source_target_pairs={{0,8},{4,12},{8,0},{12,4},{16,24},{20,28},{24,16},{28,20},{1,9},{5... | collective-permute-start | bytes 3145736 | tf_op jit(solution)/shard_map/ppermute | solution.py:28
  14.4 26.0 %collective-permute-start.2 = (bf16[2048,256]{1,0:T(8,128)(2,1)}, bf16[2048,256]{1,0:T(8,128)(2,1)}, u32[]{:S(2)}, u32[]{:S(2)}) collective-permute-start(bf16[2048,256]{1,0:T(8,128)(2,1)} %cut.1.after_ref), channel_id=1, source_target_pairs={{0,16},{4,20},{8,24},{12,28},{16,0},{20,4},{24,8},{28,12},{1,17},{... | collective-permute-start | bytes 3145736 | tf_op jit(solution)/shard_map/ppermute | solution.py:28
  15.9 0.6 copy-start.6
  53.3 14.6 %collective-permute-start.3 = (bf16[1024,256]{1,0:T(8,128)(2,1)}, bf16[1024,256]{1,0:T(8,128)(2,1)}, u32[]{:S(2)}, u32[]{:S(2)}) collective-permute-start(bf16[1024,256]{1,0:T(8,128)(2,1)} %get-tuple-element.37.refs_1_), channel_id=1, source_target_pairs={{0,16},{4,20},{8,24},{12,28},{16,0},{20,4},{24,8},{28,12},{1,17},{... | collective-permute-start | bytes 1572872 | tf_op jit(solution)/shard_map/ppermute | solution.py:28
  54.4 14.2 %collective-permute-start.4 = (bf16[1024,256]{1,0:T(8,128)(2,1)}, bf16[1024,256]{1,0:T(8,128)(2,1)}, u32[]{:S(2)}, u32[]{:S(2)}) collective-permute-start(bf16[1024,256]{1,0:T(8,128)(2,1)} %get-tuple-element.42), channel_id=1, source_target_pairs={{0,8},{4,12},{8,0},{12,4},{16,24},{20,28},{24,16},{28,20},{1,9},{5... | collective-permute-start | bytes 1572872 | tf_op jit(solution)/shard_map/ppermute | solution.py:28
  65.7 36.4 %collective-permute-start.10 = (bf16[2048,384]{1,0:T(8,128)(2,1)}, bf16[2048,384]{1,0:T(8,128)(2,1)}, u32[]{:S(2)}, u32[]{:S(2)}) collective-permute-start(bf16[2048,384]{1,0:T(8,128)(2,1)} %get-tuple-element.41.refs_0_), channel_id=1, source_target_pairs={{0,16},{4,20},{8,24},{12,28},{16,0},{20,4},{24,8},{28,12},{1,17},{... | collective-permute-start | bytes 4718600 | tf_op jit(solution)/shard_map/ppermute | solution.py:28
  66.7 36.1 %collective-permute-start.9 = (bf16[2048,384]{1,0:T(8,128)(2,1)}, bf16[2048,384]{1,0:T(8,128)(2,1)}, u32[]{:S(2)}, u32[]{:S(2)}) collective-permute-start(bf16[2048,384]{1,0:T(8,128)(2,1)} %get-tuple-element.41.refs_0_), channel_id=1, source_target_pairs={{0,8},{4,12},{8,0},{12,4},{16,24},{20,28},{24,16},{28,20},{1,9},{5... | collective-permute-start | bytes 4718600 | tf_op jit(solution)/shard_map/ppermute | solution.py:28
  67.7 5.4 %collective-permute-start.5 = (bf16[512,512]{1,0:T(8,128)(2,1)}, bf16[512,512]{1,0:T(8,128)(2,1)S(1)}, u32[]{:S(2)}, u32[]{:S(2)}) collective-permute-start(bf16[512,512]{1,0:T(8,128)(2,1)} %get-tuple-element.38.refs_0_), channel_id=1, source_target_pairs={{0,4},{4,0},{8,12},{12,8},{16,20},{20,16},{24,28},{28,24},{1,5},{5... | collective-permute-start | bytes 1572872 | tf_op jit(solution)/shard_map/ppermute | solution.py:28
  67.9 5.8 %collective-permute-start.6 = (bf16[512,512]{1,0:T(8,128)(2,1)}, bf16[512,512]{1,0:T(8,128)(2,1)}, u32[]{:S(2)}, u32[]{:S(2)}) collective-permute-start(bf16[512,512]{1,0:T(8,128)(2,1)} %get-tuple-element.39.refs_1_), channel_id=1, source_target_pairs={{0,4},{4,0},{8,12},{12,8},{16,20},{20,16},{24,28},{28,24},{1,5},{5... | collective-permute-start | bytes 1572872 | tf_op jit(solution)/shard_map/ppermute | solution.py:28
  68.6 5.0 %collective-permute-start.7 = (bf16[512,512]{1,0:T(8,128)(2,1)}, bf16[512,512]{1,0:T(8,128)(2,1)}, u32[]{:S(2)}, u32[]{:S(2)}) collective-permute-start(bf16[512,512]{1,0:T(8,128)(2,1)} %get-tuple-element.40.refs_2_), channel_id=1, source_target_pairs={{0,4},{4,0},{8,12},{12,8},{16,20},{20,16},{24,28},{28,24},{1,5},{5... | collective-permute-start | bytes 1572872 | tf_op jit(solution)/shard_map/ppermute | solution.py:28
  73.1 2.4 copy-start
  73.1 2.4 collective-permute-start.8
  84.3 110.0 %reduce-scatter.6.cloned.1.call-start = ((), (), s32[]{:S(2)}) async-start(), calls=%async_computation.4 | async-start | bytes 3932160 | tf_op jit(solution)/shard_map/reduce_scatter | solution.py:536
  106.1 20.8 %collective-permute-start.13 = (bf16[1024,384]{1,0:T(8,128)(2,1)}, bf16[1024,384]{1,0:T(8,128)(2,1)S(1)}, u32[]{:S(2)}, u32[]{:S(2)}) collective-permute-start(bf16[1024,384]{1,0:T(8,128)(2,1)} %get-tuple-element.45.refs_11_), channel_id=1, source_target_pairs={{0,16},{4,20},{8,24},{12,28},{16,0},{20,4},{24,8},{28,12},{1,17},{... | collective-permute-start | bytes 2359304 | tf_op jit(solution)/shard_map/ppermute | solution.py:28
  107.3 20.8 %collective-permute-start.14 = (bf16[1024,384]{1,0:T(8,128)(2,1)}, bf16[1024,384]{1,0:T(8,128)(2,1)}, u32[]{:S(2)}, u32[]{:S(2)}) collective-permute-start(bf16[1024,384]{1,0:T(8,128)(2,1)} %get-tuple-element.46), channel_id=1, source_target_pairs={{0,8},{4,12},{8,0},{12,4},{16,24},{20,28},{24,16},{28,20},{1,9},{5... | collective-permute-start | bytes 2359304 | tf_op jit(solution)/shard_map/ppermute | solution.py:28
  108.4 50.6 %collective-permute-start.11 = (bf16[2048,384]{1,0:T(8,128)(2,1)}, bf16[2048,384]{1,0:T(8,128)(2,1)}, u32[]{:S(2)}, u32[]{:S(2)}) collective-permute-start(bf16[2048,384]{1,0:T(8,128)(2,1)} %get-tuple-element.44), channel_id=1, source_target_pairs={{0,8},{4,12},{8,0},{12,4},{16,24},{20,28},{24,16},{28,20},{1,9},{5... | collective-permute-start | bytes 4718600 | tf_op jit(solution)/shard_map/ppermute | solution.py:28
  109.3 49.6 %collective-permute-start.12 = (bf16[2048,384]{1,0:T(8,128)(2,1)}, bf16[2048,384]{1,0:T(8,128)(2,1)}, u32[]{:S(2)}, u32[]{:S(2)}) collective-permute-start(bf16[2048,384]{1,0:T(8,128)(2,1)} %get-tuple-element.44), channel_id=1, source_target_pairs={{0,16},{4,20},{8,24},{12,28},{16,0},{20,4},{24,8},{28,12},{1,17},{... | collective-permute-start | bytes 4718600 | tf_op jit(solution)/shard_map/ppermute | solution.py:28
  126.9 1.2 copy-start.5
  133.8 123.3 %reduce-scatter.8.cloned.1.call-start = ((), (), s32[]{:S(2)}) async-start(), calls=%async_computation.5 | async-start | bytes 3932160 | tf_op jit(solution)/shard_map/reduce_scatter | solution.py:536
  161.3 17.7 %collective-permute-start.15 = (bf16[1024,384]{1,0:T(8,128)(2,1)}, bf16[1024,384]{1,0:T(8,128)(2,1)}, u32[]{:S(2)}, u32[]{:S(2)}) collective-permute-start(bf16[1024,384]{1,0:T(8,128)(2,1)} %get-tuple-element.51.refs_11_), channel_id=1, source_target_pairs={{0,16},{4,20},{8,24},{12,28},{16,0},{20,4},{24,8},{28,12},{1,17},{... | collective-permute-start | bytes 2359304 | tf_op jit(solution)/shard_map/ppermute | solution.py:28
  162.6 17.0 %collective-permute-start.16 = (bf16[1024,384]{1,0:T(8,128)(2,1)}, bf16[1024,384]{1,0:T(8,128)(2,1)}, u32[]{:S(2)}, u32[]{:S(2)}) collective-permute-start(bf16[1024,384]{1,0:T(8,128)(2,1)} %get-tuple-element.52), channel_id=1, source_target_pairs={{0,8},{4,12},{8,0},{12,4},{16,24},{20,28},{24,16},{28,20},{1,9},{5... | collective-permute-start | bytes 2359304 | tf_op jit(solution)/shard_map/ppermute | solution.py:28
  165.2 11.5 %collective-permute-start.17 = (bf16[512,256]{1,0:T(8,128)(2,1)}, bf16[512,256]{1,0:T(8,128)(2,1)S(1)}, u32[]{:S(2)}, u32[]{:S(2)}) collective-permute-start(bf16[512,256]{1,0:T(8,128)(2,1)} %get-tuple-element.57), channel_id=1, source_target_pairs={{0,4},{4,0},{8,12},{12,8},{16,20},{20,16},{24,28},{28,24},{1,5},{5... | collective-permute-start | bytes 786440 | tf_op jit(solution)/shard_map/ppermute | solution.py:28
  176.7 0.7 copy-start.3
  197.2 1.9 collective-permute-start.18
  199.2 0.8 copy-start.2
  259.9 1.9 collective-permute-start.19
  261.9 0.8 copy-start.1
Sparse Core Ops, SparseCore 0:
  84.4 44.1 reduce-scatter.3
  133.9 60.3 reduce-scatter.5
  196.7 60.2 reduce-scatter.7

commit v3 on v2

--- a/solution.py
+++ b/solution.py
@@ -17,7 +17,7 @@
 CUTS = 4
 K1COST = 60
 MIXCOST = 20
-PA, PB, PC = 0.1, 35, 50
+PA, PB, PC = 0.1, 35, 40
 VMEM = 63 * 1024 * 1024
 SMEM_SPEC = pl.BlockSpec(memory_space=pltpu.SMEM)
 ANY_SPEC = pl.BlockSpec(memory_space=pl.ANY)
@@ -157,9 +157,9 @@
 
 
 def mix_kernel(
-    count, cut, mine_ref, q_ref, halo_ref, taps_ref, rates_ref, y_ref, entry_ref, ends_ref, *refs
+    cut, mine_ref, q_ref, halo_ref, taps_ref, rates_ref, y_ref, entry_ref, ends_ref, *refs
 ):
-    outs, (q_rows, mixed_rows) = refs[-2 - count - cut : -2 - cut], refs[-2:]
+    out, (q_rows, mixed_rows) = refs[-3 - cut], refs[-2:]
     if cut:
         refs[-3][...] = refs[0][...]
     rows, width = q_ref.shape[1], q_ref.shape[2]
@@ -205,12 +205,7 @@
             return q1, q2, carried
 
         lax.fori_loop(0, length // unroll, steps, (pick(-1), pick(-2), carried))
-        for step, out in enumerate(outs):
-
-            @pl.when(pl.program_id(0) == step)
-            def _():
-                out[:, lanes] = mixed_rows[...].astype(out.dtype)
-
+        out[:, lanes] = mixed_rows[...].astype(out.dtype)
         return 0
 
     lax.fori_loop(0, width // LANES, group, 0)
@@ -232,8 +227,8 @@
         pl.BlockSpec((order, SUB, tile), lambda c: (0, 0, first + c)),
         pl.BlockSpec((ends.shape[0], order, tile), lambda c: (0, 0, first + c)),
     ]
-    out_specs = [pl.BlockSpec((rows, tile), lambda c: (0, 0))] * count
-    out_shape = [jax.ShapeDtypeStruct((rows, tile), BF16)] * count
+    out_specs = [pl.BlockSpec((rows, tile), lambda c: (0, c))]
+    out_shape = [jax.ShapeDtypeStruct((rows, count * tile), BF16)]
     args = [mine, projected, halo, taps, rates, y, entry, ends]
     if cut:
         w, column, columns = cut
@@ -248,7 +243,7 @@
         out_shape.append(jax.ShapeDtypeStruct((w.shape[0], columns), BF16))
         args.append(w)
     return pl.pallas_call(
-        functools.partial(mix_kernel, count, cut is not None),
+        functools.partial(mix_kernel, cut is not None),
         grid=(count,),
         in_specs=in_specs + [ANY_SPEC] * len(after),
         out_specs=out_specs,
@@ -318,36 +313,34 @@
     )(*arrays, *after)
 
 
-def project_kernel(first, parts, slot_ref, *refs):
-    sides = [
-        jnp.concatenate([ref[...] for ref in refs[side * TILES : (side + 1) * TILES]], axis=1)
-        for side in range(2)
-    ]
-    refs = refs[2 * TILES :]
-    weights, (out_ref, token_ref) = refs[: sum(parts)], refs[-2:]
+def project_kernel(first, groups, parts, sides, slot_ref, *refs):
+    out_ref, token_ref = refs[-2:]
     token_ref[...] = jnp.zeros(token_ref.shape, F32)
-    at = 0
-    for piece, count in enumerate(parts):
-        for side, tokens in enumerate(sides):
+    refs = iter(refs)
+    tokens = [jnp.concatenate([next(refs)[...] for _ in range(count)], axis=1) for count in groups]
+    weights = [[[next(refs) for _ in range(count)] for count in piece] for piece in parts]
+    for piece in range(len(parts[0])):
+        for side, (which, whose) in enumerate(sides):
             result = None
             low = 0
-            for part in weights[at : at + count]:
+            for part in weights[whose][piece]:
                 depth = part.shape[0]
-                term = jnp.dot(tokens[:, low : low + depth], part[...], preferred_element_type=F32)
+                term = jnp.dot(tokens[which][:, low : low + depth], part[...], preferred_element_type=F32)
                 result = term if result is None else result + term
                 low += depth
             out_ref[piece ^ slot_ref[0] if first else 0, side] = result.astype(BF16)
-        at += count
-
-
-def project_part(slot, own, other, pieces, column, width, weight, out, count, after):
-    rows, depth = own[0].shape
-    parts = [len(piece) for piece in pieces]
-    weights = [part for piece in pieces for part in piece]
+
+
+def project_part(slot, tokens, weights, column, width, weight, out, count, after):
+    sides = [(0, 0), (len(tokens) - 1, len(weights) - 1)]
+    rows = tokens[0][0].shape[0]
     steps = 2
     tile = rows // steps
-    in_specs = [pl.BlockSpec((tile, depth), lambda i, slot_ref: (i, 0))] * (2 * TILES)
-    for i, part in enumerate(weights):
+    in_specs = [
+        pl.BlockSpec((tile, part.shape[1]), lambda i, slot_ref: (i, 0)) for group in tokens for part in group
+    ]
+    flat = [part for pieces in weights for piece in pieces for part in piece]
+    for i, part in enumerate(flat):
         if i == 0 and out is None:
             in_specs.append(
                 pl.BlockSpec(
@@ -356,7 +349,7 @@
             )
         else:
             in_specs.append(pl.BlockSpec(part.shape, lambda i, slot_ref: (0, 0)))
-    args = [*own, *other, *weights, *after]
+    args = [*(part for group in tokens for part in group), *flat, *after]
     in_specs += [ANY_SPEC] * len(after)
     aliases = {}
     if out is None:
@@ -368,8 +361,10 @@
         aliases = {1 + len(args): 0}
         in_specs.append(ANY_SPEC)
         args.append(out)
-    return pl.pallas_call(
-        functools.partial(project_kernel, out is None, parts),
+    groups = [len(group) for group in tokens]
+    parts = [[len(piece) for piece in pieces] for pieces in weights]
+    return pl.pallas_call(
+        functools.partial(project_kernel, out is None, groups, parts, sides),
         grid_spec=pltpu.PrefetchScalarGridSpec(
             num_scalar_prefetch=1,
             grid=(steps,),
@@ -403,16 +398,16 @@
 
     def column(i, side_ref):
         which = side_ref[0] if landed is None else 1 - side_ref[0]
-        return (0, which * half + first // LANES + i)
+        return (0, pl.multiple_of((which * half + first // LANES) * LANES, LANES))
 
     if landed is None:
-        in_specs = [pl.BlockSpec((2, rows, LANES), lambda i, side_ref: (0, 0, i))]
+        in_specs = [pl.BlockSpec((2, rows, width), lambda i, side_ref: (0, 0, 0))]
     else:
-        in_specs = [pl.BlockSpec((rows, LANES), lambda i, side_ref: (0, i))]
-    out_specs = [pl.BlockSpec((rows, LANES), column)]
+        in_specs = [pl.BlockSpec((rows, width), lambda i, side_ref: (0, 0))]
+    out_specs = [pl.BlockSpec((pl.Element(rows), pl.Element(width)), column)]
     out_shape = [jax.ShapeDtypeStruct(shape, BF16)]
     if landed is None:
-        out_specs.append(pl.BlockSpec((rows, LANES), lambda i, side_ref: (0, i)))
+        out_specs.append(pl.BlockSpec((rows, width), lambda i, side_ref: (0, 0)))
         out_shape.append(jax.ShapeDtypeStruct((rows, width), BF16))
     args, aliases = [strip], {}
     if out is not None:
@@ -423,7 +418,7 @@
         place_both_kernel if landed is None else place_kernel,
         grid_spec=pltpu.PrefetchScalarGridSpec(
             num_scalar_prefetch=1,
-            grid=(width // LANES,),
+            grid=(1,),
             in_specs=in_specs,
             out_specs=out_specs,
         ),
@@ -433,6 +428,34 @@
         cost_estimate=cost(0.2, 8),
         name="place",
     )(side, *args)
+
+
+def place_last_kernel(side_ref, sums_ref, *refs):
+    refs[-1][...] = sums_ref[0]
+
+
+def place_last(side, sums, first, out):
+    rows, half = out.shape[0], out.shape[1] // 2 // LANES
+    width = sums.shape[-1]
+
+    def column(i, side_ref):
+        which = side_ref[0] ^ i
+        return (0, pl.multiple_of((which * half + first // LANES) * LANES, LANES))
+
+    return pl.pallas_call(
+        place_last_kernel,
+        grid_spec=pltpu.PrefetchScalarGridSpec(
+            num_scalar_prefetch=1,
+            grid=(2,),
+            in_specs=[pl.BlockSpec((1, rows, width), lambda i, side_ref: (i, 0, 0)), ANY_SPEC],
+            out_specs=pl.BlockSpec((pl.Element(rows), pl.Element(width)), column),
+        ),
+        out_shape=jax.ShapeDtypeStruct(out.shape, BF16),
+        input_output_aliases={2: 0},
+        compiler_params=params(),
+        cost_estimate=cost(0.2, 8),
+        name="place",
+    )(side, sums, out)
 
 
 def body(projected, short_weight, rates, residues, bias, out_weight):
@@ -460,20 +483,20 @@
     def first_hops(sent):
         return swap(sent, "ctx", near), swap(sent, "ctx", far)
 
-    def second_hops(s, arrived, after, then=True):
+    def second_hops(s, arrived, after):
         half, cols = depth // 2, (0, widths[s])
         sources = [(arrived[0], (0, half), cols), (arrived[1], (half, half), cols)]
-        if then and s + 1 < stages:
+        if s + 1 < stages:
             sources.append(cut_of(s + 1))
         low, high, *sent = copy_part(sources, after, "pass_weights")
         diagonal = [swap(low, "ctx", far), swap(high, "ctx", near)]
-        return low, diagonal, first_hops(sent[0]) if sent else None
+        return low, diagonal, sent[0] if sent else None
 
     def pieces_of(s, arrived, diagonal):
         pieces = {
             0: [out_weight],
-            near: [arrived[0]],
-            far: [arrived[1]],
+            near: arrived[0] if isinstance(arrived[0], list) else [arrived[0]],
+            far: arrived[1] if isinstance(arrived[1], list) else [arrived[1]],
             near | far: list(diagonal),
         }
         for mask in more:
@@ -484,16 +507,21 @@
         return [pieces[r] for r in sorted(pieces)]
 
     last = projected[:, rows - 2 :, :]
-    halo = from_behind(last, "ctx")
-    (sent,) = copy_part([cut_of(0)], [last], "cut")
-    arrived = first_hops(sent)
-    y, entry, end = local_part(projected, halo, short_weight, rates, residues, bias[None], sent)
-    ends = lax.all_gather(join_part(end, arrived), "ctx")
-    token, diagonal, _ = second_hops(0, arrived, [ends], then=False)
+    sent = copy_part(
+        [(out_weight, (top, depth // 2), (starts[0], widths[0])) for top in (0, depth // 2)], [last], "cut"
+    )
+    halo = from_behind(join_part(last, sent), "ctx")
+    hops = [swap(part, "ctx", mask) for mask in (near, far) for part in sent]
+    y, entry, end = local_part(projected, halo, short_weight, rates, residues, bias[None], sent[0])
+    ends = lax.all_gather(join_part(end, hops), "ctx")
+    low_top = join_part(hops[0], [ends])
+    high_bottom = join_part(hops[3], [ends])
+    diagonal = [swap(low_top, "ctx", far), swap(high_bottom, "ctx", near)]
+    arrived = [[low_top, hops[1]], [hops[2], high_bottom]]
     early = TILES - 1
     *mixed, sent = mix_part(
         mine.astype(jnp.int32)[None], projected, halo, short_weight, rates, y, entry, ends,
-        range(early), (out_weight, starts[1], widths[1]), [token],
+        range(early), (out_weight, starts[1], widths[1]), [],
     )
     upcoming = first_hops(sent)
     mixed += mix_part(
@@ -513,30 +541,40 @@
 
     for s in range(stages):
         if s > 0:
-            arrived = upcoming
-            token, diagonal, upcoming = second_hops(s, arrived, [token, *sums[: s - 1]])
+            arrived, cut = upcoming, sent
+            token, diagonal, sent = second_hops(s, arrived, [token, *sums[: s - 1]])
+            upcoming = first_hops(sent) if s + 1 < stages else None
+        if s > 0 and s + 1 == stages:
+            arrived = [join_part(part, [token]) for part in arrived]
+            cut = join_part(cut, [token])
         pieces = pieces_of(s, arrived, diagonal)
         weight = (PA, PB, PC)[s]
+        if s + 1 < stages:
+            tokens, weights = [mixed, other], [pieces]
+        else:
+            theirs = [[swap(part, "ctx", 1) for part in piece] for piece in [[cut], *pieces[1:-1]]]
+            tokens, weights = [mixed], [pieces, [*theirs, None]]
         if s == 0:
             partial, token = project_part(
-                slot, mixed, other, pieces, starts[s], widths[s], weight, None, groups, [token]
+                slot, tokens, weights, starts[s], widths[s], weight, None, groups, [token]
             )
         else:
             partial, token = project_part(
-                slot, mixed, other, pieces[:-1], starts[s], widths[s], 0.1, None, groups, [token]
+                slot, tokens, [part[:-1] for part in weights], starts[s], widths[s], 0.1, None, groups, [token]
             )
+            if s + 1 == stages:
+                held = [join_part(part, [token]) for part in pieces[-1]]
+                weights = [[held], [[swap(part, "ctx", 1) for part in held]]]
             partial, token = project_part(
-                slot, mixed, other, pieces[-1:], starts[s], widths[s], weight, partial, groups, [token]
+                slot, tokens, [part[-1:] for part in weights], starts[s], widths[s], weight, partial, groups, [token]
             )
-        if s == stages - 1:
-            out = place_stage(0, None)
-            partial = join_part(partial, [sums[-1], out])
-        elif s > 0:
+        if s > 0:
             partial = join_part(partial, sums[-1:])
         sums.append(lax.psum_scatter(partial, "ch", scatter_dimension=0))
-    for s in range(1, stages):
+    out = None
+    for s in range(stages - 1):
         out = place_stage(s, out)
-    return out
+    return place_last(side, sums[-1], starts[-1], out)
 
 
 def solution(mesh):

time: 272 us -> 264 us (0.971)
  Pallas kernels: 102 us -> 94.2 us
    reduce_scatter x3, waiting for transfers between devices: 63.7 us -> 51.4 us  [body(): sums.append(lax.psum_scatter(partial, 'ch', scatter_dimension=0))]
    ppermute x19 -> x23, waiting for transfers between devices: 60.5 us -> 70.2 us  [swap(): return lax.ppermute(value, axis, [(i, i ^ mask) for i in range(count)])]
    pallas_call x6 -> x4, Pallas kernels: 14.4 us -> 7.34 us  [place_part(): pl.pallas_call(place_both_kernel if landed is None else place_kernel, gri...]
    pallas_call x4 -> x3, Pallas kernels: 9.7 us -> 7.72 us  [copy_part(): pl.pallas_call(functools.partial(copy_kernel, places), in_specs=[ANY_SPEC...]
    pallas_call x7 -> x8, Pallas kernels: 57.7 us -> 59.1 us  [the longest x5 42.8 us: project_part(): pl.pallas_call(functools.partial(project_kernel, out is None, groups, par...]
    ppermute x19 -> x23, starting transfers between devices: 15.3 us -> 15.7 us  [swap(): return lax.ppermute(value, axis, [(i, i ^ mask) for i in range(count)])]
  transfers between devices with their start and end apart: 23 -> 27, of which waited for: 15 -> 21; matrix products, arithmetic and copies ran while one was open for 0% -> 0% of each run, Pallas kernels for 35% -> 34%
where the time goes in v3:
time: 264 us
  waiting for transfers between devices  122 us (46%)
  Pallas kernels  94.2 us (36%)
  starting transfers between devices  18.3 us (7%)
  between operations  13.3 us (5%)
  blocking collectives  10.8 us (4%)
  local copies, waits for them, and re-layouts  5.28 us (2%)
    ppermute x23, waiting for transfers between devices, swap(): return lax.ppermute(value, axis, [(i, i ^ mask) for i in range(count)])  70.2 us
    reduce_scatter x3, waiting for transfers between devices, body(): sums.append(lax.psum_scatter(partial, 'ch', scatter_dimension=0))  51.4 us
    pallas_call x5, Pallas kernels, project_part(): pl.pallas_call(functools.partial(project_kernel, out is None, groups, par...  42.8 us
    pallas_call x1, Pallas kernels, local_part(): pl.pallas_call(local_kernel, grid=(width // tile,), in_specs=[pl.BlockSpe...  20 us
    ppermute x23, starting transfers between devices, swap(): return lax.ppermute(value, axis, [(i, i ^ mask) for i in range(count)])  15.7 us
    pallas_call x2, Pallas kernels, mix_part(): pl.pallas_call(functools.partial(mix_kernel, cut is not None), grid=(coun...  14.4 us
    all_gather x1, blocking collectives, body(): ends = lax.all_gather(join_part(end, hops), 'ctx')  10.8 us
    pallas_call x3, Pallas kernels, copy_part(): pl.pallas_call(functools.partial(copy_kernel, places), in_specs=[ANY_SPEC...  7.72 us
  transfers between devices with their start and end apart: 27, of which 21 were waited for; matrix products, arithmetic and copies ran while one was open for 0% of the time, Pallas kernels for 34%

profile of v3, /device:TPU:0, one launch (start us, length us, event | category | flops | bytes accessed | tf_op | source)
XLA Modules:
  0.0 263.5 jit_solution(17089235934571327859)
XLA Ops:
  6.5 1.5 slice.3.refs_2_.refs_0_
  8.1 2.1 cut.1
  10.2 2.4 collective-permute-start
  12.6 2.6 collective-permute-start.1
  15.2 1.5 collective-permute-start.3
  17.9 20.0 %local_conv.1 = (f32[64,8,2048]{2,1,0:T(8,128)}, f32[16,8,2048]{2,1,0:T(8,128)}, bf16[16,2048]{1,0:T(8,128)(2,1)}) custom-call(bf16[3,512,2048]{2,1,0:T(8,128)(2,1)} %q_ref.3, bf16[3,512,2048]{2,1,0:T(8,128)(2,1)} %q_ref.3, bf16[3,2,2048]{2,1,0:T(2,128)(2,1)} %copy-done.8, f32[3,3,2048]{2,1,0:T(4,128)} %taps_ref.5, f32[16,2048]{1,0:T(8,128)} %rates_ref.5, ...), custom_call_target="tpu_custom_call" | custom-call | flops 60000002048 | bytes 12582912 | tf_op jit(solution)/shard_map/local_conv/pallas_call | solution.py:125
  38.7 2.5 collective-permute-done.4.refs_4_.refs_0_
  41.2 10.8 %all-gather = bf16[128,2048]{1,0:T(8,128)(2,1)} all-gather(bf16[16,2048]{1,0:T(8,128)(2,1)} %join.12), channel_id=2, replica_groups=mesh['ctx'=8,'ch'=4] {'ctx'}, dimensions={0}, use_global_device_ids=true | all-gather | bytes 589824 | tf_op jit(solution)/shard_map/all_gather | solution.py:516
  52.0 1.1 collective-permute-start.5
  53.0 1.0 collective-permute-start.6
  54.0 9.9 %mix.2 = (bf16[512,1536]{1,0:T(8,128)(2,1)}, bf16[2048,384]{1,0:T(8,128)(2,1)}) custom-call(s32[1]{0:T(128)} %bitcast.2.mine_ref, bf16[3,512,2048]{2,1,0:T(8,128)(2,1)} %q_ref.3, bf16[3,2,2048]{2,1,0:T(2,128)(2,1)} %copy-done.8, f32[3,3,2048]{2,1,0:T(4,128)} %taps_ref.5, f32[16,2048]{1,0:T(8,128)} %rates_ref.5, f32[64,8,2048]{2,1,0:T(8,128)} %get-tuple-element.32.y_ref, ...), custom_call_target="tpu_custom_call" | custom-call | flops 20000000000 | bytes 8 | tf_op jit(solution)/shard_map/mix/pallas_call | solution.py:245
  63.9 1.1 collective-permute-start.7
  64.9 1.0 collective-permute-start.8
  66.4 1.5 collective-permute-done.6.refs_2_.refs_10_
  67.9 4.5 %mix.3.refs_1_.refs_11_ = bf16[512,512]{1,0:T(8,128)(2,1)} custom-call(s32[1]{0:T(128)} %bitcast.2.mine_ref, bf16[3,512,2048]{2,1,0:T(8,128)(2,1)} %q_ref.3, bf16[3,2,2048]{2,1,0:T(2,128)(2,1)} %copy-done.8, f32[3,3,2048]{2,1,0:T(4,128)} %taps_ref.5, f32[16,2048]{1,0:T(8,128)} %rates_ref.5, f32[64,8,2048]{2,1,0:T(8,128)} %get-tuple-element.32.y_ref, ...), custom_call_target="tpu_custom_call" | custom-call | flops 20000000000 | bytes 8 | tf_op jit(solution)/shard_map/mix/pallas_call | solution.py:245
  72.4 2.1 collective-permute-done.10.refs_3_
  75.4 8.6 %project.5 = (bf16[4,2,512,256]{3,2,1,0:T(8,128)(2,1)}, f32[8,128]{1,0:T(8,128)}) custom-call(s32[1]{0:T(128)} %bitcast.1.slot_ref, bf16[512,1536]{1,0:T(8,128)(2,1)} %get-tuple-element.35.refs_0_, bf16[512,512]{1,0:T(8,128)(2,1)} %mix.3.refs_1_.refs_11_, bf16[512,1536]{1,0:T(8,128)(2,1)} %collective-permute-done.9.refs_2_, bf16[512,512]{1,0:T(8,128)(2,1)} %copy-done.2, ...), custom_call_target="tpu_custom_call" | custom-call | flops 100000000 | bytes 8 | tf_op jit(solution)/shard_map/project/pallas_call | solution.py:366
  84.0 17.0 %collective-permute-done.7.refs_0_.refs_5_ = bf16[2048,384]{1,0:T(8,128)(2,1)} collective-permute-done((bf16[2048,384]{1,0:T(8,128)(2,1)}, bf16[2048,384]{1,0:T(8,128)(2,1)}, u32[]{:S(2)}, u32[]{:S(2)}) %collective-permute-start.7) | collective-permute-done | bytes 1572896 | tf_op jit(solution)/shard_map/ppermute | solution.py:28
  101.1 3.3 %pass_weights.2 = (bf16[1024,384]{1,0:T(8,128)(2,1)}, bf16[1024,384]{1,0:T(8,128)(2,1)}, bf16[2048,384]{1,0:T(8,128)(2,1)}) custom-call(bf16[2048,384]{1,0:T(8,128)(2,1)} %collective-permute-done.7.refs_0_.refs_5_, bf16[2048,384]{1,0:T(8,128)(2,1)} %collective-permute-done.8.refs_1_.refs_6_, bf16[2048,1024]{1,0:T(8,128)(2,1)} %refs_2_.3, ...), custom_call_target="tpu_custom_call" | custom-call | flops 100000000 | bytes 8 | tf_op jit(solution)/shard_map/pass_weights/pallas_call | solution.py:303
  104.3 1.0 collective-permute-start.13
  105.4 1.1 collective-permute-start.14
  106.4 1.0 collective-permute-start.11
  107.4 1.1 collective-permute-start.12
  108.5 11.2 %project.6 = (bf16[4,2,512,384]{3,2,1,0:T(8,128)(2,1)}, f32[8,128]{1,0:T(8,128)}) custom-call(s32[1]{0:T(128)} %bitcast.1.slot_ref, bf16[512,1536]{1,0:T(8,128)(2,1)} %get-tuple-element.35.refs_0_, bf16[512,512]{1,0:T(8,128)(2,1)} %mix.3.refs_1_.refs_11_, bf16[512,1536]{1,0:T(8,128)(2,1)} %collective-permute-done.9.refs_2_, bf16[512,512]{1,0:T(8,128)(2,1)} %copy-done.2, ...), custom_call_target="tpu_custom_call" | custom-call | flops 100000000 | bytes 8 | tf_op jit(solution)/shard_map/project/pallas_call | solution.py:366
  119.7 5.4 %collective-permute-done.13.refs_4_ = bf16[1024,384]{1,0:T(8,128)(2,1)S(1)} collective-permute-done((bf16[1024,384]{1,0:T(8,128)(2,1)}, bf16[1024,384]{1,0:T(8,128)(2,1)S(1)}, u32[]{:S(2)}, u32[]{:S(2)}) %collective-permute-start.13) | collective-permute-done | bytes 786464 | tf_op jit(solution)/shard_map/ppermute | solution.py:28
  125.1 1.1 collective-permute-done.14.refs_5_
  126.2 5.4 %project.7 = (bf16[4,2,512,384]{3,2,1,0:T(8,128)(2,1)}, f32[8,128]{1,0:T(8,128)}) custom-call(s32[1]{0:T(128)} %bitcast.1.slot_ref, bf16[512,1536]{1,0:T(8,128)(2,1)} %get-tuple-element.35.refs_0_, bf16[512,512]{1,0:T(8,128)(2,1)} %mix.3.refs_1_.refs_11_, bf16[512,1536]{1,0:T(8,128)(2,1)} %collective-permute-done.9.refs_2_, ...), custom_call_target="tpu_custom_call", output_to_operand_aliasing={{0}: (8, {})} | custom-call | flops 35000000512 | bytes 8 | tf_op jit(solution)/shard_map/project/pallas_call | solution.py:366
  131.8 26.1 %collective-permute-done.11.refs_0_ = bf16[2048,384]{1,0:T(8,128)(2,1)} collective-permute-done((bf16[2048,384]{1,0:T(8,128)(2,1)}, bf16[2048,384]{1,0:T(8,128)(2,1)}, u32[]{:S(2)}, u32[]{:S(2)}) %collective-permute-start.11) | collective-permute-done | bytes 1572896 | tf_op jit(solution)/shard_map/ppermute | solution.py:28
  158.0 2.3 pass_weights.3
  161.0 1.0 collective-permute-start.19
  162.0 1.0 collective-permute-start.15
  163.0 1.1 collective-permute-done.16.refs_5_
  164.1 2.2 collective-permute-done.18.refs_7_
  166.4 2.2 collective-permute-done.17.refs_6_
  168.6 12.2 %project.8 = (bf16[4,2,512,384]{3,2,1,0:T(8,128)(2,1)}, f32[8,128]{1,0:T(8,128)}) custom-call(s32[1]{0:T(128)} %bitcast.1.slot_ref, bf16[512,1536]{1,0:T(8,128)(2,1)} %get-tuple-element.35.refs_0_, bf16[512,512]{1,0:T(8,128)(2,1)} %mix.3.refs_1_.refs_11_, bf16[2048,1024]{1,0:T(8,128)(2,1)} %refs_2_.3, bf16[2048,384]{1,0:T(8,128)(2,1)} %join.15.refs_3_, ...), custom_call_target="tpu_custom_call" | custom-call | flops 100000000 | bytes 8 | tf_op jit(solution)/shard_map/project/pallas_call | solution.py:366
  181.7 2.1 collective-permute-done.21.refs_5_
  183.8 1.0 collective-permute-done.20.refs_4_
  184.8 0.9 copy-done.7
  185.7 5.5 %project.9 = (bf16[4,2,512,384]{3,2,1,0:T(8,128)(2,1)}, f32[8,128]{1,0:T(8,128)}) custom-call(s32[1]{0:T(128)} %bitcast.1.slot_ref, bf16[512,1536]{1,0:T(8,128)(2,1)} %get-tuple-element.35.refs_0_, bf16[512,512]{1,0:T(8,128)(2,1)} %mix.3.refs_1_.refs_11_, bf16[1024,384]{1,0:T(8,128)(2,1)} %join.18.refs_2_, ...), custom_call_target="tpu_custom_call", output_to_operand_aliasing={{0}: (8, {})} | custom-call | flops 40000000000 | bytes 8 | tf_op jit(solution)/shard_map/project/pallas_call | solution.py:366
  191.2 1.2 reduce-scatter.6.cloned.1.call-done
  192.4 1.8 place.5
  194.3 1.7 collective-permute-done.22.refs_0_
  196.7 1.7 place.6.refs_0_
  198.4 2.1 place.7
  200.6 1.8 collective-permute-done.23.refs_0_
  203.1 1.8 place.8.refs_0_
  204.9 50.2 %reduce-scatter.8.cloned.1.call-done = bf16[1,2,512,384]{3,2,1,0:T(8,128)(2,1)} async-done(((bf16[4,2,512,384]{3,2,1,0:T(8,128)(2,1)}), bf16[1,2,512,384]{3,2,1,0:T(8,128)(2,1)}) %reduce-scatter.8.cloned.1.call-update) | async-done | bytes 786448 | tf_op jit(solution)/shard_map/reduce_scatter | solution.py:573
  255.1 1.9 place.9
  (56 shorter events, 6.9 us)
Async XLA Ops:
  6.5 125.0 %reduce-scatter.4.cloned.1.call-start = ((), (), s32[]{:S(2)}) async-start(), calls=%async_computation.3 | async-start | bytes 2621440 | tf_op jit(solution)/shard_map/reduce_scatter | solution.py:573
  10.2 7.0 %collective-permute-start = (bf16[3,2,2048]{2,1,0:T(2,128)(2,1)}, bf16[3,2,2048]{2,1,0:T(2,128)(2,1)S(1)}, u32[]{:S(2)}, u32[]{:S(2)}) collective-permute-start(bf16[3,2,2048]{2,1,0:T(2,128)(2,1)} %join.11), channel_id=1, source_target_pairs={{0,4},{4,8},{8,12},{12,16},{16,20},{20,24},{24,28},{1,5},{5,9},{9,... | collective-permute-start | bytes 73736 | tf_op jit(solution)/shard_map/ppermute | solution.py:33
  12.6 25.3 %collective-permute-start.1 = (bf16[1024,256]{1,0:T(8,128)(2,1)}, bf16[1024,256]{1,0:T(8,128)(2,1)S(1)}, u32[]{:S(2)}, u32[]{:S(2)}) collective-permute-start(bf16[1024,256]{1,0:T(8,128)(2,1)} %get-tuple-element.30.refs_1_.after_ref), channel_id=1, source_target_pairs={{0,8},{4,12},{8,0},{12,4},{16,24},{20,28},{24,16},{28,20},{1,9},{5... | collective-permute-start | bytes 1572872 | tf_op jit(solution)/shard_map/ppermute | solution.py:28
  15.2 22.7 %collective-permute-start.3 = (bf16[1024,256]{1,0:T(8,128)(2,1)}, bf16[1024,256]{1,0:T(8,128)(2,1)}, u32[]{:S(2)}, u32[]{:S(2)}) collective-permute-start(bf16[1024,256]{1,0:T(8,128)(2,1)} %get-tuple-element.30.refs_1_.after_ref), channel_id=1, source_target_pairs={{0,16},{4,20},{8,24},{12,28},{16,0},{20,4},{24,8},{28,12},{1,17},{... | collective-permute-start | bytes 1572872 | tf_op jit(solution)/shard_map/ppermute | solution.py:28
  16.7 22.0 %collective-permute-start.2 = (bf16[1024,256]{1,0:T(8,128)(2,1)}, bf16[1024,256]{1,0:T(8,128)(2,1)}, u32[]{:S(2)}, u32[]{:S(2)}) collective-permute-start(bf16[1024,256]{1,0:T(8,128)(2,1)} %get-tuple-element.31.refs_2_), channel_id=1, source_target_pairs={{0,8},{4,12},{8,0},{12,4},{16,24},{20,28},{24,16},{28,20},{1,9},{5... | collective-permute-start | bytes 1572872 | tf_op jit(solution)/shard_map/ppermute | solution.py:28
  17.2 23.9 %collective-permute-start.4 = (bf16[1024,256]{1,0:T(8,128)(2,1)}, bf16[1024,256]{1,0:T(8,128)(2,1)}, u32[]{:S(2)}, u32[]{:S(2)}) collective-permute-start(bf16[1024,256]{1,0:T(8,128)(2,1)} %get-tuple-element.31.refs_2_), channel_id=1, source_target_pairs={{0,16},{4,20},{8,24},{12,28},{16,0},{20,4},{24,8},{28,12},{1,17},{... | collective-permute-start | bytes 1572872 | tf_op jit(solution)/shard_map/ppermute | solution.py:28
  17.3 0.6 copy-start.8
  37.9 3.3 %copy-start.1 = (bf16[1024,256]{1,0:T(8,128)(2,1)}, bf16[1024,256]{1,0:T(8,128)(2,1)S(1)}, u32[]{:S(2)}) copy-start(bf16[1024,256]{1,0:T(8,128)(2,1)S(1)} %collective-permute-done.1.refs_1_.refs_0_) | copy-start | bytes 1572868
  52.0 14.4 %collective-permute-start.5 = (bf16[1024,256]{1,0:T(8,128)(2,1)}, bf16[1024,256]{1,0:T(8,128)(2,1)S(1)}, u32[]{:S(2)}, u32[]{:S(2)}) collective-permute-start(bf16[1024,256]{1,0:T(8,128)(2,1)} %join.13.refs_5_), channel_id=1, source_target_pairs={{0,16},{4,20},{8,24},{12,28},{16,0},{20,4},{24,8},{28,12},{1,17},{... | collective-permute-start | bytes 1572872 | tf_op jit(solution)/shard_map/ppermute | solution.py:28
  53.0 14.8 %collective-permute-start.6 = (bf16[1024,256]{1,0:T(8,128)(2,1)}, bf16[1024,256]{1,0:T(8,128)(2,1)}, u32[]{:S(2)}, u32[]{:S(2)}) collective-permute-start(bf16[1024,256]{1,0:T(8,128)(2,1)} %join.14.refs_8_), channel_id=1, source_target_pairs={{0,8},{4,12},{8,0},{12,4},{16,24},{20,28},{24,16},{28,20},{1,9},{5... | collective-permute-start | bytes 1572872 | tf_op jit(solution)/shard_map/ppermute | solution.py:28
  63.9 37.1 %collective-permute-start.7 = (bf16[2048,384]{1,0:T(8,128)(2,1)}, bf16[2048,384]{1,0:T(8,128)(2,1)}, u32[]{:S(2)}, u32[]{:S(2)}) collective-permute-start(bf16[2048,384]{1,0:T(8,128)(2,1)} %get-tuple-element.36.refs_0_), channel_id=1, source_target_pairs={{0,8},{4,12},{8,0},{12,4},{16,24},{20,28},{24,16},{28,20},{1,9},{5... | collective-permute-start | bytes 4718600 | tf_op jit(solution)/shard_map/ppermute | solution.py:28
  64.9 36.1 %collective-permute-start.8 = (bf16[2048,384]{1,0:T(8,128)(2,1)}, bf16[2048,384]{1,0:T(8,128)(2,1)}, u32[]{:S(2)}, u32[]{:S(2)}) collective-permute-start(bf16[2048,384]{1,0:T(8,128)(2,1)} %get-tuple-element.36.refs_0_), channel_id=1, source_target_pairs={{0,16},{4,20},{8,24},{12,28},{16,0},{20,4},{24,8},{28,12},{1,17},{... | collective-permute-start | bytes 4718600 | tf_op jit(solution)/shard_map/ppermute | solution.py:28
  65.9 8.7 %collective-permute-start.9 = (bf16[512,1536]{1,0:T(8,128)(2,1)}, bf16[512,1536]{1,0:T(8,128)(2,1)}, u32[]{:S(2)}, u32[]{:S(2)}) collective-permute-start(bf16[512,1536]{1,0:T(8,128)(2,1)} %get-tuple-element.35.refs_0_), channel_id=1, source_target_pairs={{0,4},{4,0},{8,12},{12,8},{16,20},{20,16},{24,28},{28,24},{1,5},{5... | collective-permute-start | bytes 4718600 | tf_op jit(solution)/shard_map/ppermute | solution.py:28
  66.4 1.5 copy-start.3
  72.4 2.1 collective-permute-start.10
  74.5 0.8 copy-start.2
  84.0 108.4 %reduce-scatter.6.cloned.1.call-start = ((), (), s32[]{:S(2)}) async-start(), calls=%async_computation.4 | async-start | bytes 3932160 | tf_op jit(solution)/shard_map/reduce_scatter | solution.py:573
  104.3 20.8 %collective-permute-start.13 = (bf16[1024,384]{1,0:T(8,128)(2,1)}, bf16[1024,384]{1,0:T(8,128)(2,1)S(1)}, u32[]{:S(2)}, u32[]{:S(2)}) collective-permute-start(bf16[1024,384]{1,0:T(8,128)(2,1)} %get-tuple-element.39.refs_7_), channel_id=1, source_target_pairs={{0,16},{4,20},{8,24},{12,28},{16,0},{20,4},{24,8},{28,12},{1,17},{... | collective-permute-start | bytes 2359304 | tf_op jit(solution)/shard_map/ppermute | solution.py:28
  105.4 20.8 %collective-permute-start.14 = (bf16[1024,384]{1,0:T(8,128)(2,1)}, bf16[1024,384]{1,0:T(8,128)(2,1)}, u32[]{:S(2)}, u32[]{:S(2)}) collective-permute-start(bf16[1024,384]{1,0:T(8,128)(2,1)} %get-tuple-element.40), channel_id=1, source_target_pairs={{0,8},{4,12},{8,0},{12,4},{16,24},{20,28},{24,16},{28,20},{1,9},{5... | collective-permute-start | bytes 2359304 | tf_op jit(solution)/shard_map/ppermute | solution.py:28
  106.4 51.6 %collective-permute-start.11 = (bf16[2048,384]{1,0:T(8,128)(2,1)}, bf16[2048,384]{1,0:T(8,128)(2,1)}, u32[]{:S(2)}, u32[]{:S(2)}) collective-permute-start(bf16[2048,384]{1,0:T(8,128)(2,1)} %get-tuple-element.38.refs_0_), channel_id=1, source_target_pairs={{0,8},{4,12},{8,0},{12,4},{16,24},{20,28},{24,16},{28,20},{1,9},{5... | collective-permute-start | bytes 4718600 | tf_op jit(solution)/shard_map/ppermute | solution.py:28
  107.4 50.6 %collective-permute-start.12 = (bf16[2048,384]{1,0:T(8,128)(2,1)}, bf16[2048,384]{1,0:T(8,128)(2,1)}, u32[]{:S(2)}, u32[]{:S(2)}) collective-permute-start(bf16[2048,384]{1,0:T(8,128)(2,1)} %get-tuple-element.38.refs_0_), channel_id=1, source_target_pairs={{0,16},{4,20},{8,24},{12,28},{16,0},{20,4},{24,8},{28,12},{1,17},{... | collective-permute-start | bytes 4718600 | tf_op jit(solution)/shard_map/ppermute | solution.py:28
  125.1 1.1 copy-start.6
  131.6 123.5 %reduce-scatter.8.cloned.1.call-start = ((), (), s32[]{:S(2)}) async-start(), calls=%async_computation.5 | async-start | bytes 3932160 | tf_op jit(solution)/shard_map/reduce_scatter | solution.py:573
  160.3 3.8 %collective-permute-start.16 = (bf16[2048,384]{1,0:T(8,128)(2,1)}, bf16[2048,384]{1,0:T(8,128)(2,1)}, u32[]{:S(2)}, u32[]{:S(2)}) collective-permute-start(bf16[2048,384]{1,0:T(8,128)(2,1)} %join.17), channel_id=1, source_target_pairs={{0,4},{4,0},{8,12},{12,8},{16,20},{20,16},{24,28},{28,24},{1,5},{5... | collective-permute-start | bytes 4718600 | tf_op jit(solution)/shard_map/ppermute | solution.py:28
  160.4 1.6 copy-start
  160.4 6.0 %collective-permute-start.18 = (bf16[2048,384]{1,0:T(8,128)(2,1)}, bf16[2048,384]{1,0:T(8,128)(2,1)}, u32[]{:S(2)}, u32[]{:S(2)}) collective-permute-start(bf16[2048,384]{1,0:T(8,128)(2,1)} %join.16.refs_4_), channel_id=1, source_target_pairs={{0,4},{4,0},{8,12},{12,8},{16,20},{20,16},{24,28},{28,24},{1,5},{5... | collective-permute-start | bytes 4718600 | tf_op jit(solution)/shard_map/ppermute | solution.py:28
  160.9 7.7 %collective-permute-start.17 = (bf16[2048,384]{1,0:T(8,128)(2,1)}, bf16[2048,384]{1,0:T(8,128)(2,1)}, u32[]{:S(2)}, u32[]{:S(2)}) collective-permute-start(bf16[2048,384]{1,0:T(8,128)(2,1)} %join.15.refs_3_), channel_id=1, source_target_pairs={{0,4},{4,0},{8,12},{12,8},{16,20},{20,16},{24,28},{28,24},{1,5},{5... | collective-permute-start | bytes 4718600 | tf_op jit(solution)/shard_map/ppermute | solution.py:28
  161.0 20.2 %collective-permute-start.19 = (bf16[1024,384]{1,0:T(8,128)(2,1)}, bf16[1024,384]{1,0:T(8,128)(2,1)}, u32[]{:S(2)}, u32[]{:S(2)}) collective-permute-start(bf16[1024,384]{1,0:T(8,128)(2,1)} %get-tuple-element.47), channel_id=1, source_target_pairs={{0,8},{4,12},{8,0},{12,4},{16,24},{20,28},{24,16},{28,20},{1,9},{5... | collective-permute-start | bytes 2359304 | tf_op jit(solution)/shard_map/ppermute | solution.py:28
  162.0 19.7 %collective-permute-start.15 = (bf16[1024,384]{1,0:T(8,128)(2,1)S(1)}, bf16[1024,384]{1,0:T(8,128)(2,1)}, u32[]{:S(2)}, u32[]{:S(2)}) collective-permute-start(bf16[1024,384]{1,0:T(8,128)(2,1)S(1)} %copy-done), channel_id=1, source_target_pairs={{0,16},{4,20},{8,24},{12,28},{16,0},{20,4},{24,8},{28,12},{1,17},{... | collective-permute-start | bytes 2359304 | tf_op jit(solution)/shard_map/ppermute | solution.py:28
  181.2 2.6 collective-permute-start.21
  181.7 3.1 %collective-permute-start.20 = (bf16[1024,384]{1,0:T(8,128)(2,1)}, bf16[1024,384]{1,0:T(8,128)(2,1)S(1)}, u32[]{:S(2)}, u32[]{:S(2)}) collective-permute-start(bf16[1024,384]{1,0:T(8,128)(2,1)} %join.18.refs_2_), channel_id=1, source_target_pairs={{0,4},{4,0},{8,12},{12,8},{16,20},{20,16},{24,28},{28,24},{1,5},{5... | collective-permute-start | bytes 2359304 | tf_op jit(solution)/shard_map/ppermute | solution.py:28
  184.8 0.9 copy-start.7
  194.3 1.7 collective-permute-start.22
  196.0 0.7 copy-start.5
  200.4 1.9 collective-permute-start.23
  202.4 0.8 copy-start.4
Sparse Core Ops, SparseCore 0:
  84.1 44.0 reduce-scatter.3
  131.7 60.6 reduce-scatter.5
  194.8 60.2 reduce-scatter.7

commit v4 on v3

--- a/solution.py
+++ b/solution.py
@@ -10,7 +10,7 @@
 F32 = jnp.float32
 BF16 = jnp.bfloat16
 STEPS = 2
-TILES = 4
+TILES = 8
 REACHES = (1, 2, 4)
 SUB = 8
 LANES = 128
@@ -30,7 +30,7 @@
 
 def from_behind(value, axis):
     count = lax.axis_size(axis)
-    return lax.ppermute(value, axis, [(i, i + 1) for i in range(count - 1)])
+    return lax.ppermute(value, axis, [(i, (i + 1) % count) for i in range(count)])
 
 
 def spread(row):
@@ -60,19 +60,19 @@
 
 
 def local_kernel(
-    k_ref, v_ref, halo_ref, taps_ref, rates_ref, residues_ref, bias_ref, after_ref,
+    mine_ref, k_ref, v_ref, halo_ref, taps_ref, rates_ref, residues_ref, bias_ref, after_ref,
     y_ref, entry_ref, end_ref, k_rows, v_rows, ends,
 ):
     rows, width = k_ref.shape[1], k_ref.shape[2]
     order = rates_ref.shape[0]
     length = rows // SUB
-    unroll = min(8, length)
+    unroll = min(16, length)
     sub = lax.broadcasted_iota(jnp.int32, (SUB, LANES), 0)
 
     def group(index, _):
         lanes = pl.ds(pl.multiple_of(index * LANES, LANES), LANES)
-        k_rows[pl.ds(SUB - 2, 2), :] = halo_ref[1, :, lanes].astype(F32)
-        v_rows[pl.ds(SUB - 2, 2), :] = halo_ref[2, :, lanes].astype(F32)
+        k_rows[pl.ds(SUB - 2, 2), :] = jnp.where(mine_ref[0] > 0, halo_ref[1, :, lanes].astype(F32), 0.0)
+        v_rows[pl.ds(SUB - 2, 2), :] = jnp.where(mine_ref[0] > 0, halo_ref[2, :, lanes].astype(F32), 0.0)
         k_rows[pl.ds(SUB, rows), :] = k_ref[0, :, lanes].astype(F32)
         v_rows[pl.ds(SUB, rows), :] = v_ref[0, :, lanes].astype(F32)
         rates = rates_ref[:, lanes]
@@ -117,7 +117,7 @@
     lax.fori_loop(0, width // LANES, group, 0)
 
 
-def local_part(projected, halo, taps, rates, residues, bias, after):
+def local_part(mine, projected, halo, taps, rates, residues, bias, after):
     rows, width = projected.shape[1:]
     order = rates.shape[0]
     tile = width // TILES
@@ -126,6 +126,7 @@
         local_kernel,
         grid=(width // tile,),
         in_specs=[
+            SMEM_SPEC,
             pl.BlockSpec((1, rows, tile), lambda c: (1, 0, c)),
             pl.BlockSpec((1, rows, tile), lambda c: (2, 0, c)),
             pl.BlockSpec((3, 2, tile), lambda c: (0, 0, c)),
@@ -153,7 +154,7 @@
         compiler_params=params(),
         cost_estimate=cost(K1COST, 12 * rows * width),
         name="local_conv",
-    )(projected, projected, halo, taps, rates, residues, bias, after)
+    )(mine, projected, projected, halo, taps, rates, residues, bias, after)
 
 
 def mix_kernel(
@@ -176,7 +177,7 @@
         for device in range(ends_ref.shape[0] - 1):
             later = before * across + ends_ref[device, :, lanes].astype(F32)
             before = jnp.where(device < mine_ref[0], later, before)
-        q_rows[pl.ds(SUB - 2, 2), :] = halo_ref[0, :, lanes].astype(F32)
+        q_rows[pl.ds(SUB - 2, 2), :] = jnp.where(mine_ref[0] > 0, halo_ref[0, :, lanes].astype(F32), 0.0)
         q_rows[pl.ds(SUB, rows), :] = q_ref[0, :, lanes].astype(F32)
         decay, carried = [], []
         all_decay = jnp.exp(-rates)
@@ -512,20 +513,21 @@
     )
     halo = from_behind(join_part(last, sent), "ctx")
     hops = [swap(part, "ctx", mask) for mask in (near, far) for part in sent]
-    y, entry, end = local_part(projected, halo, short_weight, rates, residues, bias[None], sent[0])
+    here = mine.astype(jnp.int32)[None]
+    y, entry, end = local_part(here, projected, halo, short_weight, rates, residues, bias[None], sent[0])
     ends = lax.all_gather(join_part(end, hops), "ctx")
     low_top = join_part(hops[0], [ends])
     high_bottom = join_part(hops[3], [ends])
     diagonal = [swap(low_top, "ctx", far), swap(high_bottom, "ctx", near)]
     arrived = [[low_top, hops[1]], [hops[2], high_bottom]]
-    early = TILES - 1
+    early = TILES * 3 // 4
     *mixed, sent = mix_part(
-        mine.astype(jnp.int32)[None], projected, halo, short_weight, rates, y, entry, ends,
+        here, projected, halo, short_weight, rates, y, entry, ends,
         range(early), (out_weight, starts[1], widths[1]), [],
     )
     upcoming = first_hops(sent)
     mixed += mix_part(
-        mine.astype(jnp.int32)[None], projected, halo, short_weight, rates, y, entry, ends,
+        here, projected, halo, short_weight, rates, y, entry, ends,
         range(early, TILES), None, [sent, *diagonal],
     )
     other = [swap(part, "ctx", 1) for part in mixed]

time: 264 us -> 263 us (level)
  no operation moved by 1% of the time
where the time goes in v4:
time: 263 us; the launch traced here: 262 us
  waiting for transfers between devices  123 us (47%)
  Pallas kernels  93.1 us (35%)
  starting transfers between devices  16.8 us (6%)
  between operations  13.3 us (5%)
  blocking collectives  10.8 us (4%)
  local copies, waits for them, and re-layouts  5.28 us (2%)
    ppermute x23, waiting for transfers between devices, swap(): return lax.ppermute(value, axis, [(i, i ^ mask) for i in range(count)])  70.9 us
    reduce_scatter x3, waiting for transfers between devices, body(): sums.append(lax.psum_scatter(partial, 'ch', scatter_dimension=0))  51.9 us
    pallas_call x5, Pallas kernels, project_part(): pl.pallas_call(functools.partial(project_kernel, out is None, groups, par...  42.9 us
    pallas_call x1, Pallas kernels, local_part(): pl.pallas_call(local_kernel, grid=(width // tile,), in_specs=[SMEM_SPEC,...  18.7 us
    ppermute x23, starting transfers between devices, swap(): return lax.ppermute(value, axis, [(i, i ^ mask) for i in range(count)])  16 us
    pallas_call x2, Pallas kernels, mix_part(): pl.pallas_call(functools.partial(mix_kernel, cut is not None), grid=(coun...  14.4 us
    all_gather x1, blocking collectives, body(): ends = lax.all_gather(join_part(end, hops), 'ctx')  10.8 us
    pallas_call x3, Pallas kernels, copy_part(): pl.pallas_call(functools.partial(copy_kernel, places), in_specs=[ANY_SPEC...  7.83 us
  transfers between devices with their start and end apart: 27, of which 21 were waited for; matrix products, arithmetic and copies ran while one was open for 0% of the time, Pallas kernels for 34%

profile of v4, /device:TPU:0, one launch (start us, length us, event | category | flops | bytes accessed | tf_op | source)
XLA Modules:
  0.0 262.0 jit_solution(2229926336732921134)
XLA Ops:
  6.5 1.5 slice.3.refs_2_.refs_0_
  8.1 2.1 cut.1
  10.7 2.6 collective-permute-start.1
  13.3 1.5 collective-permute-start.3
  16.0 18.7 %local_conv.1 = (f32[64,8,2048]{2,1,0:T(8,128)}, f32[16,8,2048]{2,1,0:T(8,128)}, bf16[16,2048]{1,0:T(8,128)(2,1)}) custom-call(s32[1]{0:T(128)} %bitcast.2.mine_ref, bf16[3,512,2048]{2,1,0:T(8,128)(2,1)} %q_ref.3, bf16[3,512,2048]{2,1,0:T(8,128)(2,1)} %q_ref.3, bf16[3,2,2048]{2,1,0:T(2,128)(2,1)} %copy-done.8, f32[3,3,2048]{2,1,0:T(4,128)} %taps_ref.5, ...), custom_call_target="tpu_custom_call" | custom-call | flops 60000002048 | bytes 12582912 | tf_op jit(solution)/shard_map/local_conv/pallas_call | solution.py:125
  34.7 2.1 collective-permute-done.2.refs_2_.refs_6_
  36.8 2.5 collective-permute-done.4.refs_4_.refs_0_
  39.4 10.8 %all-gather = bf16[128,2048]{1,0:T(8,128)(2,1)} all-gather(bf16[16,2048]{1,0:T(8,128)(2,1)} %join.12), channel_id=2, replica_groups=mesh['ctx'=8,'ch'=4] {'ctx'}, dimensions={0}, use_global_device_ids=true | all-gather | bytes 589824 | tf_op jit(solution)/shard_map/all_gather | solution.py:518
  50.2 1.0 collective-permute-start.5
  51.1 1.1 collective-permute-start.6
  52.2 10.2 %mix.2 = (bf16[512,1536]{1,0:T(8,128)(2,1)}, bf16[2048,384]{1,0:T(8,128)(2,1)}) custom-call(s32[1]{0:T(128)} %bitcast.2.mine_ref, bf16[3,512,2048]{2,1,0:T(8,128)(2,1)} %q_ref.3, bf16[3,2,2048]{2,1,0:T(2,128)(2,1)} %copy-done.8, f32[3,3,2048]{2,1,0:T(4,128)} %taps_ref.5, f32[16,2048]{1,0:T(8,128)} %rates_ref.5, f32[64,8,2048]{2,1,0:T(8,128)} %get-tuple-element.32.y_ref, ...), custom_call_target="tpu_custom_call" | custom-call | flops 20000000000 | bytes 8 | tf_op jit(solution)/shard_map/mix/pallas_call | solution.py:246
  62.4 0.9 collective-permute-start.7
  63.3 1.1 collective-permute-start.8
  64.6 0.9 collective-permute-done.6.refs_2_.refs_10_
  65.5 4.2 %mix.3.refs_1_.refs_11_ = bf16[512,512]{1,0:T(8,128)(2,1)} custom-call(s32[1]{0:T(128)} %bitcast.2.mine_ref, bf16[3,512,2048]{2,1,0:T(8,128)(2,1)} %q_ref.3, bf16[3,2,2048]{2,1,0:T(2,128)(2,1)} %copy-done.8, f32[3,3,2048]{2,1,0:T(4,128)} %taps_ref.5, f32[16,2048]{1,0:T(8,128)} %rates_ref.5, f32[64,8,2048]{2,1,0:T(8,128)} %get-tuple-element.32.y_ref, ...), custom_call_target="tpu_custom_call" | custom-call | flops 20000000000 | bytes 8 | tf_op jit(solution)/shard_map/mix/pallas_call | solution.py:246
  69.9 1.9 collective-permute-done.10.refs_3_
  71.9 0.8 copy-done.2
  72.7 8.6 %project.5 = (bf16[4,2,512,256]{3,2,1,0:T(8,128)(2,1)}, f32[8,128]{1,0:T(8,128)}) custom-call(s32[1]{0:T(128)} %bitcast.1.slot_ref, bf16[512,1536]{1,0:T(8,128)(2,1)} %get-tuple-element.35.refs_0_, bf16[512,512]{1,0:T(8,128)(2,1)} %mix.3.refs_1_.refs_11_, bf16[512,1536]{1,0:T(8,128)(2,1)} %collective-permute-done.9.refs_2_, bf16[512,512]{1,0:T(8,128)(2,1)} %copy-done.2, ...), custom_call_target="tpu_custom_call" | custom-call | flops 100000000 | bytes 8 | tf_op jit(solution)/shard_map/project/pallas_call | solution.py:367
  81.3 17.7 %collective-permute-done.7.refs_0_.refs_5_ = bf16[2048,384]{1,0:T(8,128)(2,1)} collective-permute-done((bf16[2048,384]{1,0:T(8,128)(2,1)}, bf16[2048,384]{1,0:T(8,128)(2,1)}, u32[]{:S(2)}, u32[]{:S(2)}) %collective-permute-start.7) | collective-permute-done | bytes 1572896 | tf_op jit(solution)/shard_map/ppermute | solution.py:28
  99.5 3.4 %pass_weights.2 = (bf16[1024,384]{1,0:T(8,128)(2,1)}, bf16[1024,384]{1,0:T(8,128)(2,1)}, bf16[2048,384]{1,0:T(8,128)(2,1)}) custom-call(bf16[2048,384]{1,0:T(8,128)(2,1)} %collective-permute-done.7.refs_0_.refs_5_, bf16[2048,384]{1,0:T(8,128)(2,1)} %collective-permute-done.8.refs_1_.refs_6_, bf16[2048,1024]{1,0:T(8,128)(2,1)} %refs_2_.3, ...), custom_call_target="tpu_custom_call" | custom-call | flops 100000000 | bytes 8 | tf_op jit(solution)/shard_map/pass_weights/pallas_call | solution.py:304
  102.8 1.1 collective-permute-start.13
  104.0 0.8 collective-permute-start.14
  104.8 1.2 collective-permute-start.11
  106.0 0.9 collective-permute-start.12
  107.0 11.2 %project.6 = (bf16[4,2,512,384]{3,2,1,0:T(8,128)(2,1)}, f32[8,128]{1,0:T(8,128)}) custom-call(s32[1]{0:T(128)} %bitcast.1.slot_ref, bf16[512,1536]{1,0:T(8,128)(2,1)} %get-tuple-element.35.refs_0_, bf16[512,512]{1,0:T(8,128)(2,1)} %mix.3.refs_1_.refs_11_, bf16[512,1536]{1,0:T(8,128)(2,1)} %collective-permute-done.9.refs_2_, bf16[512,512]{1,0:T(8,128)(2,1)} %copy-done.2, ...), custom_call_target="tpu_custom_call" | custom-call | flops 100000000 | bytes 8 | tf_op jit(solution)/shard_map/project/pallas_call | solution.py:367
  118.2 5.4 %collective-permute-done.13.refs_4_ = bf16[1024,384]{1,0:T(8,128)(2,1)S(1)} collective-permute-done((bf16[1024,384]{1,0:T(8,128)(2,1)}, bf16[1024,384]{1,0:T(8,128)(2,1)S(1)}, u32[]{:S(2)}, u32[]{:S(2)}) %collective-permute-start.13) | collective-permute-done | bytes 786464 | tf_op jit(solution)/shard_map/ppermute | solution.py:28
  123.6 1.2 collective-permute-done.14.refs_5_
  124.8 5.5 %project.7 = (bf16[4,2,512,384]{3,2,1,0:T(8,128)(2,1)}, f32[8,128]{1,0:T(8,128)}) custom-call(s32[1]{0:T(128)} %bitcast.1.slot_ref, bf16[512,1536]{1,0:T(8,128)(2,1)} %get-tuple-element.35.refs_0_, bf16[512,512]{1,0:T(8,128)(2,1)} %mix.3.refs_1_.refs_11_, bf16[512,1536]{1,0:T(8,128)(2,1)} %collective-permute-done.9.refs_2_, ...), custom_call_target="tpu_custom_call", output_to_operand_aliasing={{0}: (8, {})} | custom-call | flops 35000000512 | bytes 8 | tf_op jit(solution)/shard_map/project/pallas_call | solution.py:367
  130.5 25.5 %collective-permute-done.11.refs_0_ = bf16[2048,384]{1,0:T(8,128)(2,1)} collective-permute-done((bf16[2048,384]{1,0:T(8,128)(2,1)}, bf16[2048,384]{1,0:T(8,128)(2,1)}, u32[]{:S(2)}, u32[]{:S(2)}) %collective-permute-start.11) | collective-permute-done | bytes 1572896 | tf_op jit(solution)/shard_map/ppermute | solution.py:28
  156.0 2.3 pass_weights.3
  159.8 1.3 collective-permute-start.15
  161.0 1.1 collective-permute-done.16.refs_5_
  162.1 2.2 collective-permute-done.18.refs_7_
  164.4 2.2 collective-permute-done.17.refs_6_
  166.6 12.2 %project.8 = (bf16[4,2,512,384]{3,2,1,0:T(8,128)(2,1)}, f32[8,128]{1,0:T(8,128)}) custom-call(s32[1]{0:T(128)} %bitcast.1.slot_ref, bf16[512,1536]{1,0:T(8,128)(2,1)} %get-tuple-element.35.refs_0_, bf16[512,512]{1,0:T(8,128)(2,1)} %mix.3.refs_1_.refs_11_, bf16[2048,1024]{1,0:T(8,128)(2,1)} %refs_2_.3, bf16[2048,384]{1,0:T(8,128)(2,1)} %join.15.refs_3_, ...), custom_call_target="tpu_custom_call" | custom-call | flops 100000000 | bytes 8 | tf_op jit(solution)/shard_map/project/pallas_call | solution.py:367
  179.7 2.1 collective-permute-done.21.refs_5_
  181.8 1.0 collective-permute-done.20.refs_4_
  182.8 0.9 copy-done.7
  183.7 5.5 %project.9 = (bf16[4,2,512,384]{3,2,1,0:T(8,128)(2,1)}, f32[8,128]{1,0:T(8,128)}) custom-call(s32[1]{0:T(128)} %bitcast.1.slot_ref, bf16[512,1536]{1,0:T(8,128)(2,1)} %get-tuple-element.35.refs_0_, bf16[512,512]{1,0:T(8,128)(2,1)} %mix.3.refs_1_.refs_11_, bf16[1024,384]{1,0:T(8,128)(2,1)} %join.18.refs_2_, ...), custom_call_target="tpu_custom_call", output_to_operand_aliasing={{0}: (8, {})} | custom-call | flops 40000000000 | bytes 8 | tf_op jit(solution)/shard_map/project/pallas_call | solution.py:367
  189.2 1.6 reduce-scatter.6.cloned.1.call-done
  190.8 1.8 place.5
  192.7 1.7 collective-permute-done.22.refs_0_
  195.1 1.7 place.6.refs_0_
  196.8 2.1 place.7
  199.0 1.8 collective-permute-done.23.refs_0_
  201.5 1.8 place.8.refs_0_
  203.3 50.2 %reduce-scatter.8.cloned.1.call-done = bf16[1,2,512,384]{3,2,1,0:T(8,128)(2,1)} async-done(((bf16[4,2,512,384]{3,2,1,0:T(8,128)(2,1)}), bf16[1,2,512,384]{3,2,1,0:T(8,128)(2,1)}) %reduce-scatter.8.cloned.1.call-update) | async-done | bytes 786448 | tf_op jit(solution)/shard_map/reduce_scatter | solution.py:575
  253.6 1.9 place.9
  (56 shorter events, 6.7 us)
Async XLA Ops:
  6.5 123.7 %reduce-scatter.4.cloned.1.call-start = ((), (), s32[]{:S(2)}) async-start(), calls=%async_computation.3 | async-start | bytes 2621440 | tf_op jit(solution)/shard_map/reduce_scatter | solution.py:575
  10.2 5.2 %collective-permute-start = (bf16[3,2,2048]{2,1,0:T(2,128)(2,1)}, bf16[3,2,2048]{2,1,0:T(2,128)(2,1)S(1)}, u32[]{:S(2)}, u32[]{:S(2)}) collective-permute-start(bf16[3,2,2048]{2,1,0:T(2,128)(2,1)} %join.11), channel_id=1, source_target_pairs={{0,4},{4,8},{8,12},{12,16},{16,20},{20,24},{24,28},{28,0},{1,5},{5... | collective-permute-start | bytes 73736 | tf_op jit(solution)/shard_map/ppermute | solution.py:33
  10.7 23.9 %collective-permute-start.1 = (bf16[1024,256]{1,0:T(8,128)(2,1)}, bf16[1024,256]{1,0:T(8,128)(2,1)S(1)}, u32[]{:S(2)}, u32[]{:S(2)}) collective-permute-start(bf16[1024,256]{1,0:T(8,128)(2,1)} %get-tuple-element.30.refs_1_.after_ref), channel_id=1, source_target_pairs={{0,8},{4,12},{8,0},{12,4},{16,24},{20,28},{24,16},{28,20},{1,9},{5... | collective-permute-start | bytes 1572872 | tf_op jit(solution)/shard_map/ppermute | solution.py:28
  13.3 21.4 %collective-permute-start.3 = (bf16[1024,256]{1,0:T(8,128)(2,1)}, bf16[1024,256]{1,0:T(8,128)(2,1)}, u32[]{:S(2)}, u32[]{:S(2)}) collective-permute-start(bf16[1024,256]{1,0:T(8,128)(2,1)} %get-tuple-element.30.refs_1_.after_ref), channel_id=1, source_target_pairs={{0,16},{4,20},{8,24},{12,28},{16,0},{20,4},{24,8},{28,12},{1,17},{... | collective-permute-start | bytes 1572872 | tf_op jit(solution)/shard_map/ppermute | solution.py:28
  14.8 22.0 %collective-permute-start.2 = (bf16[1024,256]{1,0:T(8,128)(2,1)}, bf16[1024,256]{1,0:T(8,128)(2,1)}, u32[]{:S(2)}, u32[]{:S(2)}) collective-permute-start(bf16[1024,256]{1,0:T(8,128)(2,1)} %get-tuple-element.31.refs_2_), channel_id=1, source_target_pairs={{0,8},{4,12},{8,0},{12,4},{16,24},{20,28},{24,16},{28,20},{1,9},{5... | collective-permute-start | bytes 1572872 | tf_op jit(solution)/shard_map/ppermute | solution.py:28
  15.4 24.0 %collective-permute-start.4 = (bf16[1024,256]{1,0:T(8,128)(2,1)}, bf16[1024,256]{1,0:T(8,128)(2,1)}, u32[]{:S(2)}, u32[]{:S(2)}) collective-permute-start(bf16[1024,256]{1,0:T(8,128)(2,1)} %get-tuple-element.31.refs_2_), channel_id=1, source_target_pairs={{0,16},{4,20},{8,24},{12,28},{16,0},{20,4},{24,8},{28,12},{1,17},{... | collective-permute-start | bytes 1572872 | tf_op jit(solution)/shard_map/ppermute | solution.py:28
  15.4 0.6 copy-start.8
  34.7 4.7 %copy-start.1 = (bf16[1024,256]{1,0:T(8,128)(2,1)}, bf16[1024,256]{1,0:T(8,128)(2,1)S(1)}, u32[]{:S(2)}) copy-start(bf16[1024,256]{1,0:T(8,128)(2,1)S(1)} %collective-permute-done.1.refs_1_.refs_0_) | copy-start | bytes 1572868
  50.2 14.4 %collective-permute-start.5 = (bf16[1024,256]{1,0:T(8,128)(2,1)}, bf16[1024,256]{1,0:T(8,128)(2,1)S(1)}, u32[]{:S(2)}, u32[]{:S(2)}) collective-permute-start(bf16[1024,256]{1,0:T(8,128)(2,1)} %join.13.refs_5_), channel_id=1, source_target_pairs={{0,16},{4,20},{8,24},{12,28},{16,0},{20,4},{24,8},{28,12},{1,17},{... | collective-permute-start | bytes 1572872 | tf_op jit(solution)/shard_map/ppermute | solution.py:28
  51.1 14.4 %collective-permute-start.6 = (bf16[1024,256]{1,0:T(8,128)(2,1)}, bf16[1024,256]{1,0:T(8,128)(2,1)}, u32[]{:S(2)}, u32[]{:S(2)}) collective-permute-start(bf16[1024,256]{1,0:T(8,128)(2,1)} %join.14.refs_8_), channel_id=1, source_target_pairs={{0,8},{4,12},{8,0},{12,4},{16,24},{20,28},{24,16},{28,20},{1,9},{5... | collective-permute-start | bytes 1572872 | tf_op jit(solution)/shard_map/ppermute | solution.py:28
  62.4 36.7 %collective-permute-start.7 = (bf16[2048,384]{1,0:T(8,128)(2,1)}, bf16[2048,384]{1,0:T(8,128)(2,1)}, u32[]{:S(2)}, u32[]{:S(2)}) collective-permute-start(bf16[2048,384]{1,0:T(8,128)(2,1)} %get-tuple-element.36.refs_0_), channel_id=1, source_target_pairs={{0,8},{4,12},{8,0},{12,4},{16,24},{20,28},{24,16},{28,20},{1,9},{5... | collective-permute-start | bytes 4718600 | tf_op jit(solution)/shard_map/ppermute | solution.py:28
  63.3 36.1 %collective-permute-start.8 = (bf16[2048,384]{1,0:T(8,128)(2,1)}, bf16[2048,384]{1,0:T(8,128)(2,1)}, u32[]{:S(2)}, u32[]{:S(2)}) collective-permute-start(bf16[2048,384]{1,0:T(8,128)(2,1)} %get-tuple-element.36.refs_0_), channel_id=1, source_target_pairs={{0,16},{4,20},{8,24},{12,28},{16,0},{20,4},{24,8},{28,12},{1,17},{... | collective-permute-start | bytes 4718600 | tf_op jit(solution)/shard_map/ppermute | solution.py:28
  64.4 7.5 %collective-permute-start.9 = (bf16[512,1536]{1,0:T(8,128)(2,1)}, bf16[512,1536]{1,0:T(8,128)(2,1)}, u32[]{:S(2)}, u32[]{:S(2)}) collective-permute-start(bf16[512,1536]{1,0:T(8,128)(2,1)} %get-tuple-element.35.refs_0_), channel_id=1, source_target_pairs={{0,4},{4,0},{8,12},{12,8},{16,20},{20,16},{24,28},{28,24},{1,5},{5... | collective-permute-start | bytes 4718600 | tf_op jit(solution)/shard_map/ppermute | solution.py:28
  64.6 0.9 copy-start.3
  69.7 2.1 collective-permute-start.10
  71.9 0.8 copy-start.2
  81.3 109.5 %reduce-scatter.6.cloned.1.call-start = ((), (), s32[]{:S(2)}) async-start(), calls=%async_computation.4 | async-start | bytes 3932160 | tf_op jit(solution)/shard_map/reduce_scatter | solution.py:575
  102.8 20.8 %collective-permute-start.13 = (bf16[1024,384]{1,0:T(8,128)(2,1)}, bf16[1024,384]{1,0:T(8,128)(2,1)S(1)}, u32[]{:S(2)}, u32[]{:S(2)}) collective-permute-start(bf16[1024,384]{1,0:T(8,128)(2,1)} %get-tuple-element.39.refs_7_), channel_id=1, source_target_pairs={{0,16},{4,20},{8,24},{12,28},{16,0},{20,4},{24,8},{28,12},{1,17},{... | collective-permute-start | bytes 2359304 | tf_op jit(solution)/shard_map/ppermute | solution.py:28
  104.0 20.8 %collective-permute-start.14 = (bf16[1024,384]{1,0:T(8,128)(2,1)}, bf16[1024,384]{1,0:T(8,128)(2,1)}, u32[]{:S(2)}, u32[]{:S(2)}) collective-permute-start(bf16[1024,384]{1,0:T(8,128)(2,1)} %get-tuple-element.40), channel_id=1, source_target_pairs={{0,8},{4,12},{8,0},{12,4},{16,24},{20,28},{24,16},{28,20},{1,9},{5... | collective-permute-start | bytes 2359304 | tf_op jit(solution)/shard_map/ppermute | solution.py:28
  104.8 51.2 %collective-permute-start.11 = (bf16[2048,384]{1,0:T(8,128)(2,1)}, bf16[2048,384]{1,0:T(8,128)(2,1)}, u32[]{:S(2)}, u32[]{:S(2)}) collective-permute-start(bf16[2048,384]{1,0:T(8,128)(2,1)} %get-tuple-element.38.refs_0_), channel_id=1, source_target_pairs={{0,8},{4,12},{8,0},{12,4},{16,24},{20,28},{24,16},{28,20},{1,9},{5... | collective-permute-start | bytes 4718600 | tf_op jit(solution)/shard_map/ppermute | solution.py:28
  106.0 50.0 %collective-permute-start.12 = (bf16[2048,384]{1,0:T(8,128)(2,1)}, bf16[2048,384]{1,0:T(8,128)(2,1)}, u32[]{:S(2)}, u32[]{:S(2)}) collective-permute-start(bf16[2048,384]{1,0:T(8,128)(2,1)} %get-tuple-element.38.refs_0_), channel_id=1, source_target_pairs={{0,16},{4,20},{8,24},{12,28},{16,0},{20,4},{24,8},{28,12},{1,17},{... | collective-permute-start | bytes 4718600 | tf_op jit(solution)/shard_map/ppermute | solution.py:28
  123.6 1.2 copy-start.6
  130.3 123.3 %reduce-scatter.8.cloned.1.call-start = ((), (), s32[]{:S(2)}) async-start(), calls=%async_computation.5 | async-start | bytes 3932160 | tf_op jit(solution)/shard_map/reduce_scatter | solution.py:575
  158.3 3.8 %collective-permute-start.16 = (bf16[2048,384]{1,0:T(8,128)(2,1)}, bf16[2048,384]{1,0:T(8,128)(2,1)}, u32[]{:S(2)}, u32[]{:S(2)}) collective-permute-start(bf16[2048,384]{1,0:T(8,128)(2,1)} %join.17), channel_id=1, source_target_pairs={{0,4},{4,0},{8,12},{12,8},{16,20},{20,16},{24,28},{28,24},{1,5},{5... | collective-permute-start | bytes 4718600 | tf_op jit(solution)/shard_map/ppermute | solution.py:28
  158.4 1.4 copy-start
  158.4 6.0 %collective-permute-start.18 = (bf16[2048,384]{1,0:T(8,128)(2,1)}, bf16[2048,384]{1,0:T(8,128)(2,1)}, u32[]{:S(2)}, u32[]{:S(2)}) collective-permute-start(bf16[2048,384]{1,0:T(8,128)(2,1)} %join.16.refs_4_), channel_id=1, source_target_pairs={{0,4},{4,0},{8,12},{12,8},{16,20},{20,16},{24,28},{28,24},{1,5},{5... | collective-permute-start | bytes 4718600 | tf_op jit(solution)/shard_map/ppermute | solution.py:28
  158.9 7.7 %collective-permute-start.17 = (bf16[2048,384]{1,0:T(8,128)(2,1)}, bf16[2048,384]{1,0:T(8,128)(2,1)}, u32[]{:S(2)}, u32[]{:S(2)}) collective-permute-start(bf16[2048,384]{1,0:T(8,128)(2,1)} %join.15.refs_3_), channel_id=1, source_target_pairs={{0,4},{4,0},{8,12},{12,8},{16,20},{20,16},{24,28},{28,24},{1,5},{5... | collective-permute-start | bytes 4718600 | tf_op jit(solution)/shard_map/ppermute | solution.py:28
  159.0 20.2 %collective-permute-start.19 = (bf16[1024,384]{1,0:T(8,128)(2,1)}, bf16[1024,384]{1,0:T(8,128)(2,1)}, u32[]{:S(2)}, u32[]{:S(2)}) collective-permute-start(bf16[1024,384]{1,0:T(8,128)(2,1)} %get-tuple-element.47), channel_id=1, source_target_pairs={{0,8},{4,12},{8,0},{12,4},{16,24},{20,28},{24,16},{28,20},{1,9},{5... | collective-permute-start | bytes 2359304 | tf_op jit(solution)/shard_map/ppermute | solution.py:28
  159.8 19.8 %collective-permute-start.15 = (bf16[1024,384]{1,0:T(8,128)(2,1)S(1)}, bf16[1024,384]{1,0:T(8,128)(2,1)}, u32[]{:S(2)}, u32[]{:S(2)}) collective-permute-start(bf16[1024,384]{1,0:T(8,128)(2,1)S(1)} %copy-done), channel_id=1, source_target_pairs={{0,16},{4,20},{8,24},{12,28},{16,0},{20,4},{24,8},{28,12},{1,17},{... | collective-permute-start | bytes 2359304 | tf_op jit(solution)/shard_map/ppermute | solution.py:28
  179.2 2.6 %collective-permute-start.21 = (bf16[1024,384]{1,0:T(8,128)(2,1)}, bf16[1024,384]{1,0:T(8,128)(2,1)}, u32[]{:S(2)}, u32[]{:S(2)}) collective-permute-start(bf16[1024,384]{1,0:T(8,128)(2,1)} %join.19.refs_3_), channel_id=1, source_target_pairs={{0,4},{4,0},{8,12},{12,8},{16,20},{20,16},{24,28},{28,24},{1,5},{5... | collective-permute-start | bytes 2359304 | tf_op jit(solution)/shard_map/ppermute | solution.py:28
  179.6 3.2 %collective-permute-start.20 = (bf16[1024,384]{1,0:T(8,128)(2,1)}, bf16[1024,384]{1,0:T(8,128)(2,1)S(1)}, u32[]{:S(2)}, u32[]{:S(2)}) collective-permute-start(bf16[1024,384]{1,0:T(8,128)(2,1)} %join.18.refs_2_), channel_id=1, source_target_pairs={{0,4},{4,0},{8,12},{12,8},{16,20},{20,16},{24,28},{28,24},{1,5},{5... | collective-permute-start | bytes 2359304 | tf_op jit(solution)/shard_map/ppermute | solution.py:28
  182.8 0.9 copy-start.7
  192.7 1.7 collective-permute-start.22
  194.4 0.7 copy-start.5
  198.9 1.9 collective-permute-start.23
  200.8 0.8 copy-start.4
Sparse Core Ops, SparseCore 0:
  81.4 44.3 reduce-scatter.3
  130.4 60.3 reduce-scatter.5
  193.2 60.2 reduce-scatter.7
